TPU v7x, 32 devices: a whole 2x2x4 slice. The times are simulated.
32 devices in a mesh: groups: 2 (over y), ffn: 4 (over z), mp: 4 (over x, core).
Axes of the slice: x: 2, y: 2, z: 4, core: 2. Of those that a mesh axis runs over, the one named last changes fastest.
Arguments:
- tokens: bfloat16 [64, 8192], P(('groups', 'ffn'), 'mp'), parts along dimension 0, may hold values from -6 to 6
- gate_weight: bfloat16 [8192, 26624], P('mp', 'ffn'), may hold values from -0.0625 to 0.0625
- up_weight: bfloat16 [8192, 26624], P('mp', 'ffn'), may hold values from -0.0625 to 0.0625
- down_weight: bfloat16 [26624, 8192], P('ffn', 'mp'), may hold values from -0.0390625 to 0.0390625
Outputs:
- block_out: bfloat16 [64, 8192], P(('groups', 'ffn'), 'mp'), parts along dimension 0
There are 2 independent parts, one for each index of `groups`. A program takes and returns all parts, laid end to end along the dimension named above; an argument that names none is the same for every part. Nothing has to cross between parts.
All inputs are finite; a program needn't handle non-finite values.
Results may differ from a plain program's by a relative error of at most 0.0049.
Values may be sent and summed in bfloat16 or wider, within the bound.
No kernel may reach another device: no remote copies, remote signals or barrier semaphores. Data moves between devices by JAX's collectives and lax.ppermute only.
A program may use at most 192 MiB of HBM per device.

v0:
```python
import jax
import jax.numpy as jnp
from jax import lax
from jax.sharding import PartitionSpec as P


def per_device(tokens, gate_weight, up_weight, down_weight):
    width = gate_weight.shape[1]
    piece = lax.all_gather(tokens, "ffn", axis=0, tiled=True)
    gate_part = jnp.dot(piece, gate_weight, preferred_element_type=jnp.float32)
    up_part = jnp.dot(piece, up_weight, preferred_element_type=jnp.float32)
    partial_sums = jnp.concatenate([gate_part, up_part], axis=1)
    summed = lax.psum(partial_sums, "mp")
    hidden = (jax.nn.silu(summed[:, :width]) * summed[:, width:]).astype(jnp.bfloat16)
    total = lax.psum_scatter(
        jnp.dot(hidden, down_weight, preferred_element_type=jnp.float32),
        "ffn",
        scatter_dimension=0,
        tiled=True,
    )
    return total.astype(jnp.bfloat16)


def solution(mesh):
    in_specs = (P(("groups", "ffn"), "mp"), P("mp", "ffn"), P("mp", "ffn"), P("ffn", "mp"))
    out_specs = P(("groups", "ffn"), "mp")
    return jax.shard_map(
        per_device, mesh=mesh, in_specs=in_specs, out_specs=out_specs, check_vma=False
    )
```

profile of v0, /device:TPU:0, one launch (start us, length us, event | category | flops | bytes accessed | tf_op | source)
XLA Modules:
  0.0 134.9 jit_solution(7411118189012299050)
XLA Ops:
  6.5 0.0 all-reduce.2.cloned.1.call-start
  6.5 15.3 %all_gather.3 = bf16[32,2048]{1,0:T(8,128)(2,1)S(1)} all-gather(bf16[8,2048]{1,0:T(8,128)(2,1)} %param.4), channel_id=1, replica_groups=mesh['groups'=2,'ffn'=4,'mp'=4] {'ffn'}, dimensions={0}, use_global_device_ids=true | all-gather | bytes 163840 | tf_op jit(solution)/shard_map/all_gather | solution.py:9
  21.8 11.2 %fusion.6 = f32[32,6656]{1,0:T(8,128)S(1)} fusion(bf16[32,2048]{1,0:T(8,128)(2,1)S(1)} %all_gather.3, bf16[2048,6656]{1,0:T(8,128)(2,1)} %param.6), kind=kOutput, calls=%fused_computation.7 | convolution fusion | flops 872415232 | bytes 28246016 | tf_op jit(solution)/shard_map/dot_general | solution.py:11
  33.0 11.2 %fusion.5 = f32[32,6656]{1,0:T(8,128)S(1)} fusion(bf16[32,2048]{1,0:T(8,128)(2,1)S(1)} %all_gather.3, bf16[2048,6656]{1,0:T(8,128)(2,1)} %param.5), kind=kOutput, calls=%fused_computation.6 | convolution fusion | flops 872415232 | bytes 28246016 | tf_op jit(solution)/shard_map/dot_general | solution.py:10
  44.1 1.3 pad_maximum_fusion
  45.4 0.0 all-reduce.2.cloned.1.call-update
  45.5 0.0 reduce-scatter.2.cloned.1.call-start
  45.5 46.4 %all-reduce.2.cloned.1.call-done = f32[32,13312]{1,0:T(8,128)} async-done(((f32[32,13312]{1,0:T(8,128)}), f32[32,13312]{1,0:T(8,128)}) %all-reduce.2.cloned.1.call-update) | async-done | bytes 1703952 | tf_op jit(solution)/shard_map/psum | solution.py:13
  91.9 14.8 %fusion.1 = f32[32,2048]{1,0:T(8,128)} fusion(bf16[6656,2048]{1,0:T(8,128)(2,1)} %param.7, f32[32,13312]{1,0:T(8,128)} %all-reduce.2.cloned.1.call-done), kind=kOutput, calls=%fused_computation.3 | convolution fusion | flops 873693184 | bytes 29229056 | tf_op jit(solution)/shard_map/dot_general | solution.py:16
  106.7 0.0 reduce-scatter.2.cloned.1.call-update
  106.7 19.9 %reduce-scatter.2.cloned.1.call-done = f32[8,2048]{1,0:T(8,128)} async-done(((f32[32,2048]{1,0:T(8,128)}), f32[8,2048]{1,0:T(8,128)}) %reduce-scatter.2.cloned.1.call-update) | async-done | bytes 65552 | tf_op jit(solution)/shard_map/reduce_scatter | solution.py:15
  126.6 1.5 %convert_element_type.7 = bf16[8,2048]{1,0:T(8,128)(2,1)} convert(f32[8,2048]{1,0:T(8,128)} %reduce-scatter.2.cloned.1.call-done) | non-fusion elementwise | flops 16384 | bytes 98304 | tf_op jit(solution)/shard_map/convert_element_type | solution.py:21
Async XLA Ops:
  6.5 85.4 %all-reduce.2.cloned.1.call-start = ((), (), s32[]{:S(2)}) async-start(), calls=%async_computation.1 | async-start | bytes 3407872 | tf_op jit(solution)/shard_map/psum | solution.py:13
  45.5 81.2 %reduce-scatter.2.cloned.1.call-start = ((), (), s32[]{:S(2)}) async-start(), calls=%async_computation.2 | async-start | bytes 327680 | tf_op jit(solution)/shard_map/reduce_scatter | solution.py:15
Sparse Core Ops, SparseCore 0:
  45.6 46.3 all-reduce.1
  106.9 19.7 reduce-scatter.1
where the time goes:
time: 135 us
  waiting for transfers between devices  66.4 us (49%)
  matrix products  37.1 us (27%)
  blocking collectives  15.3 us (11%)
  between operations  13.4 us (10%)
  other arithmetic  2.75 us (2%)
    psum x1, waiting for transfers between devices, per_device(): summed = lax.psum(partial_sums, 'mp')  46.4 us
    reduce_scatter x1, waiting for transfers between devices, per_device(): lax.psum_scatter(jnp.dot(hidden, down_weight, preferred_element_type=jnp....  19.9 us
    all_gather x1, blocking collectives, per_device(): piece = lax.all_gather(tokens, 'ffn', axis=0, tiled=True)  15.3 us
    dot_general x1, matrix products, per_device(): jnp.dot(hidden, down_weight, preferred_element_type=jnp.float32)  14.8 us
    dot_general x1, matrix products, per_device(): gate_part = jnp.dot(piece, gate_weight, preferred_element_type=jnp.float32)  11.2 us
    dot_general x1, matrix products, per_device(): up_part = jnp.dot(piece, up_weight, preferred_element_type=jnp.float32)  11.2 us
  transfers between devices with their start and end apart: 2, of which 2 were waited for; matrix products, arithmetic and copies ran while one was open for 0% of the time, Pallas kernels for 0%

commit v1 on v0

v1 whole, which is shorter than its diff:
```python
import jax
import jax.numpy as jnp
from jax import lax
from jax.experimental import pallas as pl
from jax.experimental.pallas import tpu as pltpu
from jax.sharding import PartitionSpec as P

BF16 = jnp.bfloat16
F32 = jnp.float32
VMEM = pl.BlockSpec(memory_space=pltpu.VMEM)
ANY = pl.BlockSpec(memory_space=pl.ANY)
COST = pl.CostEstimate(flops=1000, bytes_accessed=1000, transcendentals=0)


def in_hbm(array):
    return pltpu.with_memory_space_constraint(array, pltpu.HBM)


def flip(size, bit):
    return [(i, i ^ bit) for i in range(size)]


def step(name, body, ins, outs, fetches, deps=()):
    n_in, n_out, n_fetch = len(ins), len(outs), len(fetches)
    n_sems = sum(pieces for *_, pieces in fetches)

    def kernel(*refs):
        in_refs, refs = refs[:n_in], refs[n_in:]
        sources, refs = refs[:n_fetch], refs[n_fetch + len(deps) :]
        out_refs, refs = refs[:n_out], refs[n_out:]
        targets, refs = refs[:n_fetch], refs[n_fetch:]
        core = lax.rem(lax.axis_index("mp"), 2)
        copies = []
        for (_, height, width, place, pieces), source, target in zip(fetches, sources, targets):
            row, column = place(core)
            tall = height // pieces
            for i in range(pieces):
                copies.append(
                    pltpu.make_async_copy(
                        source.at[
                            pl.ds(pl.multiple_of(row + i * tall, 16), tall),
                            pl.ds(pl.multiple_of(column, 128), width),
                        ],
                        target.at[pl.ds(i * tall, tall)],
                        refs[0].at[len(copies)],
                    )
                )
        for copy in copies:
            copy.start()
        if body is not None:
            body(in_refs, out_refs)
        for copy in copies:
            copy.wait()

    out_shape = tuple(pltpu.VMEM(shape, dtype) for shape, dtype in outs)
    out_shape += tuple(pltpu.VMEM((height, width), BF16) for _, height, width, _, _ in fetches)
    return pl.pallas_call(
        kernel,
        out_shape=out_shape,
        in_specs=[VMEM] * n_in + [ANY] * (n_fetch + len(deps)),
        out_specs=(VMEM,) * (n_out + n_fetch),
        scratch_shapes=[pltpu.SemaphoreType.DMA((n_sems,))] if n_sems else [],
        compiler_params=pltpu.CompilerParams(vmem_limit_bytes=3 << 20),
        cost_estimate=COST,
        name=name,
    )(*ins, *(in_hbm(weight) for weight, *_ in fetches), *deps)


def gate_up_body(refs, out_refs):
    x_ref, gate_ref, up_ref = refs
    (out_ref,) = out_refs
    width = gate_ref.shape[1]
    x = x_ref[...]
    for base, weight in ((0, gate_ref), (width, up_ref)):
        for c in range(0, width, 256):
            got = jnp.dot(x, weight[:, c : c + 256], preferred_element_type=F32)
            out_ref[:, base + c : base + c + 256] = got.astype(out_ref.dtype)


def down_body(refs, out_refs):
    *so_far, own_ref, other_ref, w_own, w_other = refs
    for c in range(0, w_own.shape[1], 256):
        got = jnp.dot(own_ref[...], w_own[:, c : c + 256], preferred_element_type=F32)
        got += jnp.dot(other_ref[...], w_other[:, c : c + 256], preferred_element_type=F32)
        for ref in so_far:
            got += ref[:, c : c + 256]
        part = got.shape[0] // len(out_refs)
        for k, ref in enumerate(out_refs):
            ref[:, c : c + 256] = got[k * part : (k + 1) * part].astype(ref.dtype)


def plain(tokens, gate_weight, up_weight, down_weight):
    width = gate_weight.shape[1]
    piece = lax.all_gather(tokens, "ffn", axis=0, tiled=True)
    gate_part = jnp.dot(piece, gate_weight, preferred_element_type=F32)
    up_part = jnp.dot(piece, up_weight, preferred_element_type=F32)
    summed = lax.psum(jnp.concatenate([gate_part, up_part], axis=1), "mp")
    hidden = (jax.nn.silu(summed[:, :width]) * summed[:, width:]).astype(BF16)
    total = lax.psum_scatter(
        jnp.dot(hidden, down_weight, preferred_element_type=F32), "ffn", scatter_dimension=0, tiled=True
    )
    return total.astype(BF16)


def ringed(n_ffn, n_mp, tokens, gate_weight, up_weight, down_weight):
    depth, columns = gate_weight.shape[0], down_weight.shape[1]
    rows = tokens.shape[0] * n_ffn
    half = gate_weight.shape[1] // 2
    first = (half // 256 + 1) // 2 * 256
    chunks = [(0, first), (first, half - first)]

    def shift(array, k):
        return lax.ppermute(array, "ffn", [(i, (i + k) % n_ffn) for i in range(n_ffn)])

    def wide(weight, chunk, mine):
        at, width = chunks[chunk]
        return weight, depth, width, lambda core: (0, (core if mine else 1 - core) * half + at), 4

    def tall(chunk, mine):
        at, height = chunks[chunk]
        return down_weight, height, columns, lambda core: ((core if mine else 1 - core) * half + at, 0), 4

    def sums(chunk, dtype):
        return (rows, 2 * chunks[chunk][1]), dtype

    def core_swap(array):
        return lax.ppermute(array, "mp", flip(n_mp, 1))

    def cross(array):
        return lax.ppermute(array, "mp", flip(n_mp, 2))

    def hidden_of(total, crossed):
        width = total.shape[1] // 2
        total = total + crossed.astype(F32)
        return (jax.nn.silu(total[:, :width]) * total[:, width:]).astype(BF16)

    gathered = [tokens] + [shift(tokens, k) for k in range(1, n_ffn)]
    g1s, u1s, g1k = step(
        "fetch", None, [], [], [wide(gate_weight, 0, False), wide(up_weight, 0, False), wide(gate_weight, 0, True)]
    )
    x = jnp.concatenate(gathered, axis=0)
    send1, u1k = step("send_0", gate_up_body, [x, g1s, u1s], [sums(0, BF16)], [wide(up_weight, 0, True)])
    got1 = core_swap(send1)
    keep1, g2s, u2s = step(
        "keep_0",
        gate_up_body,
        [x, g1k, u1k],
        [sums(0, F32)],
        [wide(gate_weight, 1, False), wide(up_weight, 1, False)],
    )
    sum1 = keep1 + got1.astype(F32)
    out1 = sum1.astype(BF16)
    crossed1 = cross(out1)
    send2, g2k, u2k = step(
        "send_1",
        gate_up_body,
        [x, g2s, u2s],
        [sums(1, BF16)],
        [wide(gate_weight, 1, True), wide(up_weight, 1, True)],
        [out1],
    )
    got2 = core_swap(send2)
    keep2, d1k = step("keep_1", gate_up_body, [x, g2k, u2k], [sums(1, F32)], [tall(0, True)])
    sum2 = keep2 + got2.astype(F32)
    out2 = sum2.astype(BF16)
    crossed2 = cross(out2)
    h1 = hidden_of(sum1, crossed1)
    (d1s,) = step("fetch_down", None, [], [], [tall(0, False)], [out2])
    h1_other = core_swap(h1)
    so_far, d2k, d2s = step(
        "down_0",
        down_body,
        [h1, h1_other, d1k, d1s],
        [((rows, columns), F32)],
        [tall(1, True), tall(1, False)],
    )
    h2 = hidden_of(sum2, crossed2)
    h2_other = core_swap(h2)
    part = (tokens.shape[0], columns)
    own, *sends = step(
        "down_1",
        down_body,
        [so_far, h2, h2_other, d2k, d2s],
        [(part, F32)] + [(part, BF16)] * (n_ffn - 1),
        [],
    )
    for k, send in enumerate(sends, 1):
        own = own + shift(send, n_ffn - k).astype(F32)
    return own.astype(BF16)


def solution(mesh):
    n_ffn, n_mp = mesh.shape["ffn"], mesh.shape["mp"]

    def per_device(tokens, gate_weight, up_weight, down_weight):
        fits = n_mp == 4 and n_ffn <= 4 and gate_weight.shape[1] % 1024 == 512
        if fits and tokens.shape[0] == 8:
            return ringed(n_ffn, n_mp, tokens, gate_weight, up_weight, down_weight)
        return plain(tokens, gate_weight, up_weight, down_weight)

    in_specs = (P(("groups", "ffn"), "mp"), P("mp", "ffn"), P("mp", "ffn"), P("ffn", "mp"))
    out_specs = P(("groups", "ffn"), "mp")
    return jax.shard_map(
        per_device, mesh=mesh, in_specs=in_specs, out_specs=out_specs, check_vma=False
    )
```

time: 135 us -> 71 us (0.53)
  waiting for transfers between devices: 66.4 us -> 10.8 us
  Pallas kernels: 0 us -> 45.3 us
  matrix products: 37.1 us -> 0 us
  blocking collectives: 15.3 us -> 0 us
  between operations: 13.4 us -> 0.2 us
  starting transfers between devices: 0.04 us -> 12.8 us
  other arithmetic: 2.75 us -> 1.02 us
    psum x1 -> x0, waiting for transfers between devices: 46.4 us -> none  [per_device(): summed = lax.psum(partial_sums, 'mp')]
    pallas_call x0 -> x8, Pallas kernels: none -> 45.3 us  [step(): pl.pallas_call(kernel, out_shape=out_shape, in_specs=[VMEM] * n_in + [ANY...]
    dot_general x3 -> x0, matrix products: 37.1 us -> none  [the longest x1 14.8 us: per_device(): jnp.dot(hidden, down_weight, preferred_element_type=jnp.float32)]
    reduce_scatter x1 -> x0, waiting for transfers between devices: 19.9 us -> none  [per_device(): lax.psum_scatter(jnp.dot(hidden, down_weight, preferred_element_type=jnp....]
    all_gather x1 -> x0, blocking collectives: 15.3 us -> none  [per_device(): piece = lax.all_gather(tokens, 'ffn', axis=0, tiled=True)]
    ppermute x0 -> x12, starting transfers between devices: none -> 12.8 us  [the longest x6 9.91 us: shift(): lax.ppermute(array, 'ffn', [(i, (i + k) % n_ffn) for i in range(n_ffn)])]
    ppermute x0 -> x12, waiting for transfers between devices: none -> 10.8 us  [the longest x2 5.83 us: cross(): return lax.ppermute(array, 'mp', flip(n_mp, 2))]
  transfers between devices with their start and end apart: 2 -> 12, of which waited for: 2 -> 5; matrix products, arithmetic and copies ran while one was open for 0% -> 2% of each run, Pallas kernels for 0% -> 43%
where the time goes in v1:
time: 71 us; the launch traced here: 70.9 us
  Pallas kernels  45.3 us (64%)
  starting transfers between devices  12.8 us (18%)
  waiting for transfers between devices  10.8 us (15%)
  other arithmetic  1.02 us (1%)
  local copies, waits for them, and re-layouts  0.81 us (1%)
    pallas_call x8, Pallas kernels, step(): pl.pallas_call(kernel, out_shape=out_shape, in_specs=[VMEM] * n_in + [ANY...  45.3 us
    ppermute x6, starting transfers between devices, shift(): lax.ppermute(array, 'ffn', [(i, (i + k) % n_ffn) for i in range(n_ffn)])  9.91 us
    ppermute x2, waiting for transfers between devices, cross(): return lax.ppermute(array, 'mp', flip(n_mp, 2))  5.83 us
    ppermute x6, waiting for transfers between devices, shift(): lax.ppermute(array, 'ffn', [(i, (i + k) % n_ffn) for i in range(n_ffn)])  4.94 us
    ppermute x2, starting transfers between devices, cross(): return lax.ppermute(array, 'mp', flip(n_mp, 2))  2.09 us
  transfers between devices with their start and end apart: 12, of which 5 were waited for; matrix products, arithmetic and copies ran while one was open for 2% of the time, Pallas kernels for 43%

profile of v1, /device:TPU:0, one launch (start us, length us, event | category | flops | bytes accessed | tf_op | source)
XLA Modules:
  0.0 70.9 jit_solution(13919331469752190717)
XLA Ops:
  0.0 4.0 %collective-permute-start.1 = (bf16[8,2048]{1,0:T(8,128)(2,1)}, bf16[8,2048]{1,0:T(8,128)(2,1)S(1)}, u32[]{:S(2)}, u32[]{:S(2)}) collective-permute-start(bf16[8,2048]{1,0:T(8,128)(2,1)} %param.4), channel_id=1, source_target_pairs={{0,8},{4,12},{8,0},{12,4},{1,9},{5,13},{9,1},{13,5},{2,10},{6,14},... | collective-permute-start | bytes 98312 | tf_op jit(solution)/shard_map/ppermute | solution.py:113
  4.0 1.6 %collective-permute-start = (bf16[8,2048]{1,0:T(8,128)(2,1)}, bf16[8,2048]{1,0:T(8,128)(2,1)S(1)}, u32[]{:S(2)}, u32[]{:S(2)}) collective-permute-start(bf16[8,2048]{1,0:T(8,128)(2,1)} %param.4), channel_id=1, source_target_pairs={{0,4},{4,8},{8,12},{12,0},{1,5},{5,9},{9,13},{13,1},{2,6},{6,10},{... | collective-permute-start | bytes 98312 | tf_op jit(solution)/shard_map/ppermute | solution.py:113
  5.6 2.2 %collective-permute-start.2 = (bf16[8,2048]{1,0:T(8,128)(2,1)}, bf16[8,2048]{1,0:T(8,128)(2,1)S(1)}, u32[]{:S(2)}, u32[]{:S(2)}) collective-permute-start(bf16[8,2048]{1,0:T(8,128)(2,1)} %param.4), channel_id=1, source_target_pairs={{0,12},{4,0},{8,4},{12,8},{1,13},{5,1},{9,5},{13,9},{2,14},{6,2},{... | collective-permute-start | bytes 98312 | tf_op jit(solution)/shard_map/ppermute | solution.py:113
  7.9 0.8 %constant_dynamic-update-slice_fusion.3 = bf16[32,2048]{1,0:T(8,128)(2,1)S(1)} fusion(bf16[8,2048]{1,0:T(8,128)(2,1)} %param.4), kind=kLoop, calls=%fused_computation.14 | loop fusion | bytes 65536
  8.7 7.5 %fetch.1 = (bf16[2048,1792]{1,0:T(8,128)(2,1)S(1)}, bf16[2048,1792]{1,0:T(8,128)(2,1)S(1)}, bf16[2048,1792]{1,0:T(8,128)(2,1)S(1)}) custom-call(bf16[2048,6656]{1,0:T(8,128)(2,1)} %refs_3_.6, bf16[2048,6656]{1,0:T(8,128)(2,1)} %refs_4_.4, bf16[2048,6656]{1,0:T(8,128)(2,1)} %refs_3_.6), custom_call_target="tpu_custom_call" | custom-call | flops 1000 | bytes 1000 | tf_op jit(solution)/shard_map/fetch/pallas_call | solution.py:57
  16.2 0.0 collective-permute-done
  16.2 0.0 collective-permute-done.1
  16.2 0.0 collective-permute-done.2
  16.3 5.7 %send_0.1 = (bf16[32,3584]{1,0:T(8,128)(2,1)S(1)}, bf16[2048,1792]{1,0:T(8,128)(2,1)S(1)}) custom-call(bf16[32,2048]{1,0:T(8,128)(2,1)S(1)} %constant_dynamic-update-slice_fusion.refs_0_, bf16[2048,1792]{1,0:T(8,128)(2,1)S(1)} %get-tuple-element.26.refs_1_, bf16[2048,1792]{1,0:T(8,128)(2,1)S(1)} %get-tuple-element.27.refs_2_, bf16[2048,6656]{1,0:T(8,128)(2,1)} %refs_4_.4), custom_call_target="tpu_custom_call" | custom-call | flops 1000 | bytes 1000 | tf_op jit(solution)/shard_map/send_0/pallas_call | solution.py:57
  21.9 0.1 collective-permute-start.3
  22.0 7.4 %keep_0.1 = (f32[32,3584]{1,0:T(8,128)S(1)}, bf16[2048,1536]{1,0:T(8,128)(2,1)S(1)}, bf16[2048,1536]{1,0:T(8,128)(2,1)S(1)}) custom-call(bf16[32,2048]{1,0:T(8,128)(2,1)S(1)} %constant_dynamic-update-slice_fusion.refs_0_, bf16[2048,1792]{1,0:T(8,128)(2,1)S(1)} %get-tuple-element.25.refs_1_, bf16[2048,1792]{1,0:T(8,128)(2,1)S(1)} %get-tuple-element.28.refs_2_, ...), custom_call_target="tpu_custom_call" | custom-call | flops 1000 | bytes 1000 | tf_op jit(solution)/shard_map/keep_0/pallas_call | solution.py:57
  29.4 0.0 collective-permute-done.3
  29.4 0.1 fusion.refs_5_
  29.4 6.8 %send_1.1 = (bf16[32,3072]{1,0:T(8,128)(2,1)S(1)}, bf16[2048,1536]{1,0:T(8,128)(2,1)S(1)}, bf16[2048,1536]{1,0:T(8,128)(2,1)S(1)}) custom-call(bf16[32,2048]{1,0:T(8,128)(2,1)S(1)} %constant_dynamic-update-slice_fusion.refs_0_, bf16[2048,1536]{1,0:T(8,128)(2,1)S(1)} %get-tuple-element.31.refs_1_, bf16[2048,1536]{1,0:T(8,128)(2,1)S(1)} %get-tuple-element.32.refs_2_, ...), custom_call_target="tpu_custom_call" | custom-call | flops 1000 | bytes 1000 | tf_op jit(solution)/shard_map/send_1/pallas_call | solution.py:57
  36.3 0.6 collective-permute-start.6
  36.9 1.5 %collective-permute-start.4 = (bf16[32,3584]{1,0:T(8,128)(2,1)S(1)}, bf16[32,3584]{1,0:T(8,128)(2,1)S(1)}, u32[]{:S(2)}, u32[]{:S(2)}) collective-permute-start(bf16[32,3584]{1,0:T(8,128)(2,1)S(1)} %fusion.refs_5_), channel_id=1, source_target_pairs={{0,2},{1,3},{2,0},{3,1},{4,6},{5,7},{6,4},{7,5},{8,10},{9,11},{10,... | collective-permute-start | bytes 688136 | tf_op jit(solution)/shard_map/ppermute | solution.py:130
  38.3 5.3 %keep_1.1 = (f32[32,3072]{1,0:T(8,128)S(1)}, bf16[1792,2048]{1,0:T(8,128)(2,1)S(1)}) custom-call(bf16[32,2048]{1,0:T(8,128)(2,1)S(1)} %constant_dynamic-update-slice_fusion.refs_0_, bf16[2048,1536]{1,0:T(8,128)(2,1)S(1)} %get-tuple-element.33.refs_1_, bf16[2048,1536]{1,0:T(8,128)(2,1)S(1)} %get-tuple-element.34.refs_2_, bf16[6656,2048]{1,0:T(8,128)(2,1)} %refs_5_.1), custom_call_target="tpu_custom_call" | custom-call | flops 1000 | bytes 1000 | tf_op jit(solution)/shard_map/keep_1/pallas_call | solution.py:57
  43.6 0.0 collective-permute-done.6
  43.7 0.6 collective-permute-start.7
  44.3 0.1 collective-permute-done.4
  44.4 0.1 convert_add_fusion
  44.5 0.1 fusion.2.refs_0_
  44.6 0.1 collective-permute-start.5
  44.7 5.7 %collective-permute-done.7 = bf16[32,3072]{1,0:T(8,128)(2,1)S(1)} collective-permute-done((bf16[32,3072]{1,0:T(8,128)(2,1)S(1)}, bf16[32,3072]{1,0:T(8,128)(2,1)S(1)}, u32[]{:S(2)}, u32[]{:S(2)}) %collective-permute-start.7) | collective-permute-done | bytes 196640 | tf_op jit(solution)/shard_map/ppermute | solution.py:130
  50.4 0.1 convert_add_fusion.2
  50.4 0.1 fusion.3.refs_1_
  50.5 0.1 collective-permute-start.8
  50.6 3.2 %fetch_down.1.refs_3_ = bf16[1792,2048]{1,0:T(8,128)(2,1)S(1)} custom-call(bf16[6656,2048]{1,0:T(8,128)(2,1)} %refs_5_.1, bf16[32,3072]{1,0:T(8,128)(2,1)S(1)} %fusion.1.refs_1_), custom_call_target="tpu_custom_call" | custom-call | flops 1000 | bytes 1000 | tf_op jit(solution)/shard_map/fetch_down/pallas_call | solution.py:57
  53.8 0.0 collective-permute-done.5.refs_1_
  53.8 7.2 %down_0.1 = (f32[32,2048]{1,0:T(8,128)S(1)}, bf16[1536,2048]{1,0:T(8,128)(2,1)S(1)}, bf16[1536,2048]{1,0:T(8,128)(2,1)S(1)}) custom-call(bf16[32,1792]{1,0:T(8,128)(2,1)S(1)} %fusion.2.refs_0_, bf16[32,1792]{1,0:T(8,128)(2,1)S(1)} %collective-permute-done.5.refs_1_, bf16[1792,2048]{1,0:T(8,128)(2,1)S(1)} %get-tuple-element.35.refs_2_, ...), custom_call_target="tpu_custom_call" | custom-call | flops 1000 | bytes 1000 | tf_op jit(solution)/shard_map/down_0/pallas_call | solution.py:57
  61.0 0.0 collective-permute-done.8.refs_2_
  61.0 2.2 %down_1.1 = (f32[8,2048]{1,0:T(8,128)S(1)}, bf16[8,2048]{1,0:T(8,128)(2,1)S(1)}, bf16[8,2048]{1,0:T(8,128)(2,1)S(1)}, bf16[8,2048]{1,0:T(8,128)(2,1)S(1)}) custom-call(f32[32,2048]{1,0:T(8,128)S(1)} %get-tuple-element.38.refs_0_, bf16[32,1536]{1,0:T(8,128)(2,1)S(1)} %fusion.3.refs_1_, bf16[32,1536]{1,0:T(8,128)(2,1)S(1)} %collective-permute-done.8.refs_2_, ...), custom_call_target="tpu_custom_call" | custom-call | flops 1000 | bytes 1000 | tf_op jit(solution)/shard_map/down_1/pallas_call | solution.py:57
  63.2 0.1 collective-permute-start.9
  63.3 1.2 %collective-permute-start.10 = (bf16[8,2048]{1,0:T(8,128)(2,1)S(1)}, bf16[8,2048]{1,0:T(8,128)(2,1)S(1)}, u32[]{:S(2)}, u32[]{:S(2)}) collective-permute-start(bf16[8,2048]{1,0:T(8,128)(2,1)S(1)} %get-tuple-element.43), channel_id=1, source_target_pairs={{0,8},{4,12},{8,0},{12,4},{1,9},{5,13},{9,1},{13,5},{2,10},{6,14},... | collective-permute-start | bytes 98312 | tf_op jit(solution)/shard_map/ppermute | solution.py:113
  64.5 0.8 %collective-permute-start.11 = (bf16[8,2048]{1,0:T(8,128)(2,1)S(1)}, bf16[8,2048]{1,0:T(8,128)(2,1)S(1)}, u32[]{:S(2)}, u32[]{:S(2)}) collective-permute-start(bf16[8,2048]{1,0:T(8,128)(2,1)S(1)} %get-tuple-element.44), channel_id=1, source_target_pairs={{0,4},{4,8},{8,12},{12,0},{1,5},{5,9},{9,13},{13,1},{2,6},{6,10},{... | collective-permute-start | bytes 98312 | tf_op jit(solution)/shard_map/ppermute | solution.py:113
  65.3 1.9 %collective-permute-done.9 = bf16[8,2048]{1,0:T(8,128)(2,1)S(1)} collective-permute-done((bf16[8,2048]{1,0:T(8,128)(2,1)S(1)}, bf16[8,2048]{1,0:T(8,128)(2,1)S(1)}, u32[]{:S(2)}, u32[]{:S(2)}) %collective-permute-start.9) | collective-permute-done | bytes 32800 | tf_op jit(solution)/shard_map/ppermute | solution.py:113
  67.2 1.0 %collective-permute-done.10 = bf16[8,2048]{1,0:T(8,128)(2,1)S(1)} collective-permute-done((bf16[8,2048]{1,0:T(8,128)(2,1)S(1)}, bf16[8,2048]{1,0:T(8,128)(2,1)S(1)}, u32[]{:S(2)}, u32[]{:S(2)}) %collective-permute-start.10) | collective-permute-done | bytes 32800 | tf_op jit(solution)/shard_map/ppermute | solution.py:113
  68.1 2.1 %collective-permute-done.11 = bf16[8,2048]{1,0:T(8,128)(2,1)S(1)} collective-permute-done((bf16[8,2048]{1,0:T(8,128)(2,1)S(1)}, bf16[8,2048]{1,0:T(8,128)(2,1)S(1)}, u32[]{:S(2)}, u32[]{:S(2)}) %collective-permute-start.11) | collective-permute-done | bytes 32800 | tf_op jit(solution)/shard_map/ppermute | solution.py:113
  70.2 0.6 add_convert_fusion
  (4 shorter events, 0.1 us)
Async XLA Ops:
  0.0 16.2 %collective-permute-start.1 = (bf16[8,2048]{1,0:T(8,128)(2,1)}, bf16[8,2048]{1,0:T(8,128)(2,1)S(1)}, u32[]{:S(2)}, u32[]{:S(2)}) collective-permute-start(bf16[8,2048]{1,0:T(8,128)(2,1)} %param.4), channel_id=1, source_target_pairs={{0,8},{4,12},{8,0},{12,4},{1,9},{5,13},{9,1},{13,5},{2,10},{6,14},... | collective-permute-start | bytes 98312 | tf_op jit(solution)/shard_map/ppermute | solution.py:113
  4.0 12.1 %collective-permute-start = (bf16[8,2048]{1,0:T(8,128)(2,1)}, bf16[8,2048]{1,0:T(8,128)(2,1)S(1)}, u32[]{:S(2)}, u32[]{:S(2)}) collective-permute-start(bf16[8,2048]{1,0:T(8,128)(2,1)} %param.4), channel_id=1, source_target_pairs={{0,4},{4,8},{8,12},{12,0},{1,5},{5,9},{9,13},{13,1},{2,6},{6,10},{... | collective-permute-start | bytes 98312 | tf_op jit(solution)/shard_map/ppermute | solution.py:113
  5.6 10.6 %collective-permute-start.2 = (bf16[8,2048]{1,0:T(8,128)(2,1)}, bf16[8,2048]{1,0:T(8,128)(2,1)S(1)}, u32[]{:S(2)}, u32[]{:S(2)}) collective-permute-start(bf16[8,2048]{1,0:T(8,128)(2,1)} %param.4), channel_id=1, source_target_pairs={{0,12},{4,0},{8,4},{12,8},{1,13},{5,1},{9,5},{13,9},{2,14},{6,2},{... | collective-permute-start | bytes 98312 | tf_op jit(solution)/shard_map/ppermute | solution.py:113
  21.9 7.4 %collective-permute-start.3 = (bf16[32,3584]{1,0:T(8,128)(2,1)S(1)}, bf16[32,3584]{1,0:T(8,128)(2,1)S(1)}, u32[]{:S(2)}, u32[]{:S(2)}) collective-permute-start(bf16[32,3584]{1,0:T(8,128)(2,1)S(1)} %get-tuple-element.30), channel_id=1, source_target_pairs={{0,1},{1,0},{2,3},{3,2},{4,5},{5,4},{6,7},{7,6},{8,9},{9,8},{10,11... | collective-permute-start | bytes 688136 | tf_op jit(solution)/shard_map/ppermute | solution.py:127
  36.3 7.4 %collective-permute-start.6 = (bf16[32,3072]{1,0:T(8,128)(2,1)S(1)}, bf16[32,3072]{1,0:T(8,128)(2,1)S(1)}, u32[]{:S(2)}, u32[]{:S(2)}) collective-permute-start(bf16[32,3072]{1,0:T(8,128)(2,1)S(1)} %get-tuple-element.37), channel_id=1, source_target_pairs={{0,1},{1,0},{2,3},{3,2},{4,5},{5,4},{6,7},{7,6},{8,9},{9,8},{10,11... | collective-permute-start | bytes 589832 | tf_op jit(solution)/shard_map/ppermute | solution.py:127
  36.9 7.6 %collective-permute-start.4 = (bf16[32,3584]{1,0:T(8,128)(2,1)S(1)}, bf16[32,3584]{1,0:T(8,128)(2,1)S(1)}, u32[]{:S(2)}, u32[]{:S(2)}) collective-permute-start(bf16[32,3584]{1,0:T(8,128)(2,1)S(1)} %fusion.refs_5_), channel_id=1, source_target_pairs={{0,2},{1,3},{2,0},{3,1},{4,6},{5,7},{6,4},{7,5},{8,10},{9,11},{10,... | collective-permute-start | bytes 688136 | tf_op jit(solution)/shard_map/ppermute | solution.py:130
  43.7 6.7 %collective-permute-start.7 = (bf16[32,3072]{1,0:T(8,128)(2,1)S(1)}, bf16[32,3072]{1,0:T(8,128)(2,1)S(1)}, u32[]{:S(2)}, u32[]{:S(2)}) collective-permute-start(bf16[32,3072]{1,0:T(8,128)(2,1)S(1)} %fusion.1.refs_1_), channel_id=1, source_target_pairs={{0,2},{1,3},{2,0},{3,1},{4,6},{5,7},{6,4},{7,5},{8,10},{9,11},{10,... | collective-permute-start | bytes 589832 | tf_op jit(solution)/shard_map/ppermute | solution.py:130
  44.6 9.2 %collective-permute-start.5 = (bf16[32,1792]{1,0:T(8,128)(2,1)S(1)}, bf16[32,1792]{1,0:T(8,128)(2,1)S(1)}, u32[]{:S(2)}, u32[]{:S(2)}) collective-permute-start(bf16[32,1792]{1,0:T(8,128)(2,1)S(1)} %fusion.2.refs_0_), channel_id=1, source_target_pairs={{0,1},{1,0},{2,3},{3,2},{4,5},{5,4},{6,7},{7,6},{8,9},{9,8},{10,11... | collective-permute-start | bytes 344072 | tf_op jit(solution)/shard_map/ppermute | solution.py:127
  50.5 10.5 %collective-permute-start.8 = (bf16[32,1536]{1,0:T(8,128)(2,1)S(1)}, bf16[32,1536]{1,0:T(8,128)(2,1)S(1)}, u32[]{:S(2)}, u32[]{:S(2)}) collective-permute-start(bf16[32,1536]{1,0:T(8,128)(2,1)S(1)} %fusion.3.refs_1_), channel_id=1, source_target_pairs={{0,1},{1,0},{2,3},{3,2},{4,5},{5,4},{6,7},{7,6},{8,9},{9,8},{10,11... | collective-permute-start | bytes 294920 | tf_op jit(solution)/shard_map/ppermute | solution.py:127
  63.2 3.9 %collective-permute-start.9 = (bf16[8,2048]{1,0:T(8,128)(2,1)S(1)}, bf16[8,2048]{1,0:T(8,128)(2,1)S(1)}, u32[]{:S(2)}, u32[]{:S(2)}) collective-permute-start(bf16[8,2048]{1,0:T(8,128)(2,1)S(1)} %get-tuple-element.42), channel_id=1, source_target_pairs={{0,12},{4,0},{8,4},{12,8},{1,13},{5,1},{9,5},{13,9},{2,14},{6,2},{... | collective-permute-start | bytes 98312 | tf_op jit(solution)/shard_map/ppermute | solution.py:113
  63.3 4.8 %collective-permute-start.10 = (bf16[8,2048]{1,0:T(8,128)(2,1)S(1)}, bf16[8,2048]{1,0:T(8,128)(2,1)S(1)}, u32[]{:S(2)}, u32[]{:S(2)}) collective-permute-start(bf16[8,2048]{1,0:T(8,128)(2,1)S(1)} %get-tuple-element.43), channel_id=1, source_target_pairs={{0,8},{4,12},{8,0},{12,4},{1,9},{5,13},{9,1},{13,5},{2,10},{6,14},... | collective-permute-start | bytes 98312 | tf_op jit(solution)/shard_map/ppermute | solution.py:113
  64.5 5.7 %collective-permute-start.11 = (bf16[8,2048]{1,0:T(8,128)(2,1)S(1)}, bf16[8,2048]{1,0:T(8,128)(2,1)S(1)}, u32[]{:S(2)}, u32[]{:S(2)}) collective-permute-start(bf16[8,2048]{1,0:T(8,128)(2,1)S(1)} %get-tuple-element.44), channel_id=1, source_target_pairs={{0,4},{4,8},{8,12},{12,0},{1,5},{5,9},{9,13},{13,1},{2,6},{6,10},{... | collective-permute-start | bytes 98312 | tf_op jit(solution)/shard_map/ppermute | solution.py:113

commit v2 on v1

--- a/solution.py
+++ b/solution.py
@@ -66,27 +66,55 @@
     )(*ins, *(in_hbm(weight) for weight, *_ in fetches), *deps)
 
 
+def tiled(width, most=1024):
+    return max(t for t in range(128, most + 1, 128) if width % t == 0)
+
+
+def each_tile(width, size, body):
+    lax.fori_loop(0, width // size, lambda i, _: (body(pl.multiple_of(i * size, 128)), 0)[1], 0)
+
+
 def gate_up_body(refs, out_refs):
     x_ref, gate_ref, up_ref = refs
     (out_ref,) = out_refs
     width = gate_ref.shape[1]
-    x = x_ref[...]
+    size = tiled(width)
     for base, weight in ((0, gate_ref), (width, up_ref)):
-        for c in range(0, width, 256):
-            got = jnp.dot(x, weight[:, c : c + 256], preferred_element_type=F32)
-            out_ref[:, base + c : base + c + 256] = got.astype(out_ref.dtype)
+
+        def one(at, base=base, weight=weight):
+            got = jnp.dot(x_ref[...], weight[:, pl.ds(at, size)], preferred_element_type=F32)
+            out_ref[:, pl.ds(pl.multiple_of(base + at, 128), size)] = got.astype(out_ref.dtype)
+
+        each_tile(width, size, one)
 
 
 def down_body(refs, out_refs):
     *so_far, own_ref, other_ref, w_own, w_other = refs
-    for c in range(0, w_own.shape[1], 256):
-        got = jnp.dot(own_ref[...], w_own[:, c : c + 256], preferred_element_type=F32)
-        got += jnp.dot(other_ref[...], w_other[:, c : c + 256], preferred_element_type=F32)
+    size = 512
+
+    def one(at):
+        span = pl.ds(at, size)
+        got = jnp.dot(own_ref[...], w_own[:, span], preferred_element_type=F32)
+        got += jnp.dot(other_ref[...], w_other[:, span], preferred_element_type=F32)
         for ref in so_far:
-            got += ref[:, c : c + 256]
+            got += ref[:, span]
         part = got.shape[0] // len(out_refs)
         for k, ref in enumerate(out_refs):
-            ref[:, c : c + 256] = got[k * part : (k + 1) * part].astype(ref.dtype)
+            ref[:, span] = got[k * part : (k + 1) * part].astype(ref.dtype)
+
+    each_tile(w_own.shape[1], size, one)
+
+
+def copy_body(refs, out_refs):
+    out_refs[0][...] = refs[0][...]
+
+
+def hidden_body(refs, out_refs):
+    total_ref, crossed_ref = refs
+    width = total_ref.shape[1] // 2
+    total = total_ref[...] + crossed_ref[...].astype(F32)
+    gate = total[:, :width]
+    out_refs[0][...] = (gate / (1 + jnp.exp(-gate)) * total[:, width:]).astype(BF16)
 
 
 def plain(tokens, gate_weight, up_weight, down_weight):
@@ -129,14 +157,16 @@
     def cross(array):
         return lax.ppermute(array, "mp", flip(n_mp, 2))
 
-    def hidden_of(total, crossed):
-        width = total.shape[1] // 2
-        total = total + crossed.astype(F32)
-        return (jax.nn.silu(total[:, :width]) * total[:, width:]).astype(BF16)
-
+    def hidden_of(total, crossed, dep):
+        shape = (rows, total.shape[1] // 2)
+        return step("hidden", hidden_body, [total, crossed], [(shape, BF16)], [], [dep])[0]
+
+    tokens, g1s = step(
+        "fetch_0", copy_body, [tokens], [(tokens.shape, BF16)], [wide(gate_weight, 0, False)]
+    )
     gathered = [tokens] + [shift(tokens, k) for k in range(1, n_ffn)]
-    g1s, u1s, g1k = step(
-        "fetch", None, [], [], [wide(gate_weight, 0, False), wide(up_weight, 0, False), wide(gate_weight, 0, True)]
+    u1s, g1k = step(
+        "fetch_1", None, [], [], [wide(up_weight, 0, False), wide(gate_weight, 0, True)], [g1s]
     )
     x = jnp.concatenate(gathered, axis=0)
     send1, u1k = step("send_0", gate_up_body, [x, g1s, u1s], [sums(0, BF16)], [wide(up_weight, 0, True)])
@@ -164,8 +194,8 @@
     sum2 = keep2 + got2.astype(F32)
     out2 = sum2.astype(BF16)
     crossed2 = cross(out2)
-    h1 = hidden_of(sum1, crossed1)
     (d1s,) = step("fetch_down", None, [], [], [tall(0, False)], [out2])
+    h1 = hidden_of(sum1, crossed1, d1s)
     h1_other = core_swap(h1)
     so_far, d2k, d2s = step(
         "down_0",
@@ -174,7 +204,7 @@
         [((rows, columns), F32)],
         [tall(1, True), tall(1, False)],
     )
-    h2 = hidden_of(sum2, crossed2)
+    h2 = hidden_of(sum2, crossed2, so_far)
     h2_other = core_swap(h2)
     part = (tokens.shape[0], columns)
     own, *sends = step(

time: 71 us -> 58.5 us (0.82)
  Pallas kernels: 45.3 us -> 35.4 us
  waiting for transfers between devices: 10.8 us -> 8.19 us
    pallas_call x8 -> x11, Pallas kernels: 45.3 us -> 35.4 us  [step(): pl.pallas_call(kernel, out_shape=out_shape, in_specs=[VMEM] * n_in + [ANY...]
    ppermute x2, waiting for transfers between devices: 5.83 us -> 0.01 us  [cross(): return lax.ppermute(array, 'mp', flip(n_mp, 2))]
    ppermute x4, waiting for transfers between devices: 0.01 us -> 2.47 us  [core_swap(): return lax.ppermute(array, 'mp', flip(n_mp, 1))]
    ppermute x6, waiting for transfers between devices: 4.94 us -> 5.72 us  [shift(): lax.ppermute(array, 'ffn', [(i, (i + k) % n_ffn) for i in range(n_ffn)])]
  transfers between devices with their start and end apart: 12 -> 12, of which waited for: 5 -> 5; matrix products, arithmetic and copies ran while one was open for 2% -> 0% of each run, Pallas kernels for 43% -> 37%
where the time goes in v2:
time: 58.5 us; the launch traced here: 58.3 us
  Pallas kernels  35.4 us (61%)
  starting transfers between devices  13.1 us (22%)
  waiting for transfers between devices  8.19 us (14%)
  local copies, waits for them, and re-layouts  0.77 us (1%)
  other arithmetic  0.73 us (1%)
    pallas_call x11, Pallas kernels, step(): pl.pallas_call(kernel, out_shape=out_shape, in_specs=[VMEM] * n_in + [ANY...  35.4 us
    ppermute x6, starting transfers between devices, shift(): lax.ppermute(array, 'ffn', [(i, (i + k) % n_ffn) for i in range(n_ffn)])  10.1 us
    ppermute x6, waiting for transfers between devices, shift(): lax.ppermute(array, 'ffn', [(i, (i + k) % n_ffn) for i in range(n_ffn)])  5.72 us
    ppermute x4, waiting for transfers between devices, core_swap(): return lax.ppermute(array, 'mp', flip(n_mp, 1))  2.47 us
    ppermute x2, starting transfers between devices, cross(): return lax.ppermute(array, 'mp', flip(n_mp, 2))  2.09 us
  transfers between devices with their start and end apart: 12, of which 5 were waited for; matrix products, arithmetic and copies ran while one was open for 0% of the time, Pallas kernels for 37%

profile of v2, /device:TPU:0, one launch (start us, length us, event | category | flops | bytes accessed | tf_op | source)
XLA Modules:
  0.0 58.3 jit_solution(3865690748023057494)
XLA Ops:
  0.0 0.0 copy-start
  0.0 0.8 %copy-done = bf16[8,2048]{1,0:T(8,128)(2,1)S(1)} copy-done((bf16[8,2048]{1,0:T(8,128)(2,1)S(1)}, bf16[8,2048]{1,0:T(8,128)(2,1)}, u32[]{:S(2)}) %copy-start) | copy-done | bytes 32792
  0.8 3.2 %fetch_0.1 = (bf16[8,2048]{1,0:T(8,128)(2,1)S(1)}, bf16[2048,1792]{1,0:T(8,128)(2,1)S(1)}) custom-call(bf16[8,2048]{1,0:T(8,128)(2,1)S(1)} %copy-done, bf16[2048,6656]{1,0:T(8,128)(2,1)} %refs_3_.6), custom_call_target="tpu_custom_call" | custom-call | flops 1000 | bytes 1000 | tf_op jit(solution)/shard_map/fetch_0/pallas_call | solution.py:57
  4.0 5.1 %collective-permute-start.2 = (bf16[8,2048]{1,0:T(8,128)(2,1)S(1)}, bf16[8,2048]{1,0:T(8,128)(2,1)S(1)}, u32[]{:S(2)}, u32[]{:S(2)}) collective-permute-start(bf16[8,2048]{1,0:T(8,128)(2,1)S(1)} %get-tuple-element.26), channel_id=1, source_target_pairs={{0,12},{4,0},{8,4},{12,8},{1,13},{5,1},{9,5},{13,9},{2,14},{6,2},{... | collective-permute-start | bytes 98312 | tf_op jit(solution)/shard_map/ppermute | solution.py:141
  9.1 0.0 collective-permute-start.1
  9.1 1.0 %collective-permute-start = (bf16[8,2048]{1,0:T(8,128)(2,1)S(1)}, bf16[8,2048]{1,0:T(8,128)(2,1)S(1)}, u32[]{:S(2)}, u32[]{:S(2)}) collective-permute-start(bf16[8,2048]{1,0:T(8,128)(2,1)S(1)} %get-tuple-element.26), channel_id=1, source_target_pairs={{0,4},{4,8},{8,12},{12,0},{1,5},{5,9},{9,13},{13,1},{2,6},{6,10},{... | collective-permute-start | bytes 98312 | tf_op jit(solution)/shard_map/ppermute | solution.py:141
  10.1 5.5 %fetch_1.1 = (bf16[2048,1792]{1,0:T(8,128)(2,1)S(1)}, bf16[2048,1792]{1,0:T(8,128)(2,1)S(1)}) custom-call(bf16[2048,6656]{1,0:T(8,128)(2,1)} %refs_4_.4, bf16[2048,6656]{1,0:T(8,128)(2,1)} %refs_3_.6, bf16[2048,1792]{1,0:T(8,128)(2,1)S(1)} %get-tuple-element.27.refs_2_.refs_1_), custom_call_target="tpu_custom_call" | custom-call | flops 1000 | bytes 1000 | tf_op jit(solution)/shard_map/fetch_1/pallas_call | solution.py:57
  15.6 0.0 collective-permute-done
  15.6 0.0 collective-permute-done.1
  15.6 0.0 collective-permute-done.2
  15.7 3.2 %send_0.1 = (bf16[32,3584]{1,0:T(8,128)(2,1)S(1)}, bf16[2048,1792]{1,0:T(8,128)(2,1)S(1)}) custom-call(bf16[32,2048]{1,0:T(8,128)(2,1)S(1)} %constant_dynamic-update-slice_fusion.refs_0_, bf16[2048,1792]{1,0:T(8,128)(2,1)S(1)} %get-tuple-element.27.refs_2_.refs_1_, bf16[2048,1792]{1,0:T(8,128)(2,1)S(1)} %get-tuple-element.29.refs_2_, bf16[2048,6656]{1,0:T(8,128)(2,1)} %refs_4_.4), custom_call_target="tpu_custom_call" | custom-call | flops 1000 | bytes 1000 | tf_op jit(solution)/shard_map/send_0/pallas_call | solution.py:57
  18.9 0.1 collective-permute-start.3
  18.9 4.9 %keep_0.1 = (f32[32,3584]{1,0:T(8,128)S(1)}, bf16[2048,1536]{1,0:T(8,128)(2,1)S(1)}, bf16[2048,1536]{1,0:T(8,128)(2,1)S(1)}) custom-call(bf16[32,2048]{1,0:T(8,128)(2,1)S(1)} %constant_dynamic-update-slice_fusion.refs_0_, bf16[2048,1792]{1,0:T(8,128)(2,1)S(1)} %get-tuple-element.28.refs_1_, bf16[2048,1792]{1,0:T(8,128)(2,1)S(1)} %get-tuple-element.30.refs_2_, ...), custom_call_target="tpu_custom_call" | custom-call | flops 1000 | bytes 1000 | tf_op jit(solution)/shard_map/keep_0/pallas_call | solution.py:57
  23.9 0.0 collective-permute-done.3
  23.9 0.1 fusion.1
  23.9 4.7 %send_1.1 = (bf16[32,3072]{1,0:T(8,128)(2,1)S(1)}, bf16[2048,1536]{1,0:T(8,128)(2,1)S(1)}, bf16[2048,1536]{1,0:T(8,128)(2,1)S(1)}) custom-call(bf16[32,2048]{1,0:T(8,128)(2,1)S(1)} %constant_dynamic-update-slice_fusion.refs_0_, bf16[2048,1536]{1,0:T(8,128)(2,1)S(1)} %get-tuple-element.33.refs_1_, bf16[2048,1536]{1,0:T(8,128)(2,1)S(1)} %get-tuple-element.34.refs_2_, ...), custom_call_target="tpu_custom_call" | custom-call | flops 1000 | bytes 1000 | tf_op jit(solution)/shard_map/send_1/pallas_call | solution.py:57
  28.7 0.5 collective-permute-start.5
  29.2 1.5 %collective-permute-start.4 = (bf16[32,3584]{1,0:T(8,128)(2,1)S(1)}, bf16[32,3584]{1,0:T(8,128)(2,1)S(1)}, u32[]{:S(2)}, u32[]{:S(2)}) collective-permute-start(bf16[32,3584]{1,0:T(8,128)(2,1)S(1)} %get-tuple-element.49.refs_5_), channel_id=1, source_target_pairs={{0,2},{1,3},{2,0},{3,1},{4,6},{5,7},{6,4},{7,5},{8,10},{9,11},{10,... | collective-permute-start | bytes 688136 | tf_op jit(solution)/shard_map/ppermute | solution.py:158
  30.7 3.2 %keep_1.1 = (f32[32,3072]{1,0:T(8,128)S(1)}, bf16[1792,2048]{1,0:T(8,128)(2,1)S(1)}) custom-call(bf16[32,2048]{1,0:T(8,128)(2,1)S(1)} %constant_dynamic-update-slice_fusion.refs_0_, bf16[2048,1536]{1,0:T(8,128)(2,1)S(1)} %get-tuple-element.35.refs_1_, bf16[2048,1536]{1,0:T(8,128)(2,1)S(1)} %get-tuple-element.36.refs_2_, bf16[6656,2048]{1,0:T(8,128)(2,1)} %refs_5_.1), custom_call_target="tpu_custom_call" | custom-call | flops 1000 | bytes 1000 | tf_op jit(solution)/shard_map/keep_1/pallas_call | solution.py:57
  33.9 0.0 collective-permute-done.5
  34.0 0.6 %collective-permute-start.7 = (bf16[32,3072]{1,0:T(8,128)(2,1)S(1)}, bf16[32,3072]{1,0:T(8,128)(2,1)S(1)}, u32[]{:S(2)}, u32[]{:S(2)}) collective-permute-start(bf16[32,3072]{1,0:T(8,128)(2,1)S(1)} %get-tuple-element.47.refs_1_), channel_id=1, source_target_pairs={{0,2},{1,3},{2,0},{3,1},{4,6},{5,7},{6,4},{7,5},{8,10},{9,11},{10,... | collective-permute-start | bytes 589832 | tf_op jit(solution)/shard_map/ppermute | solution.py:158
  34.6 3.2 %fetch_down.1.refs_2_.refs_3_ = bf16[1792,2048]{1,0:T(8,128)(2,1)S(1)} custom-call(bf16[6656,2048]{1,0:T(8,128)(2,1)} %refs_5_.1, bf16[32,3072]{1,0:T(8,128)(2,1)S(1)} %get-tuple-element.47.refs_1_), custom_call_target="tpu_custom_call" | custom-call | flops 1000 | bytes 1000 | tf_op jit(solution)/shard_map/fetch_down/pallas_call | solution.py:57
  37.8 0.0 collective-permute-done.4.refs_1_
  37.8 0.1 hidden.2.refs_0_
  37.9 0.1 collective-permute-start.6
  38.0 1.3 %collective-permute-done.6.refs_1_ = bf16[32,1792]{1,0:T(8,128)(2,1)S(1)} collective-permute-done((bf16[32,1792]{1,0:T(8,128)(2,1)S(1)}, bf16[32,1792]{1,0:T(8,128)(2,1)S(1)}, u32[]{:S(2)}, u32[]{:S(2)}) %collective-permute-start.6) | collective-permute-done | bytes 114720 | tf_op jit(solution)/shard_map/ppermute | solution.py:155
  39.3 4.7 %down_0.1 = (f32[32,2048]{1,0:T(8,128)S(1)}, bf16[1536,2048]{1,0:T(8,128)(2,1)S(1)}, bf16[1536,2048]{1,0:T(8,128)(2,1)S(1)}) custom-call(bf16[32,1792]{1,0:T(8,128)(2,1)S(1)} %hidden.2.refs_0_, bf16[32,1792]{1,0:T(8,128)(2,1)S(1)} %collective-permute-done.6.refs_1_, bf16[1792,2048]{1,0:T(8,128)(2,1)S(1)} %get-tuple-element.39.refs_2_, ...), custom_call_target="tpu_custom_call" | custom-call | flops 1000 | bytes 1000 | tf_op jit(solution)/shard_map/down_0/pallas_call | solution.py:57
  44.0 0.0 collective-permute-done.7.refs_1_
  44.0 0.1 hidden.3.refs_1_
  44.1 0.2 collective-permute-start.8
  44.3 1.2 %collective-permute-done.8.refs_2_ = bf16[32,1536]{1,0:T(8,128)(2,1)S(1)} collective-permute-done((bf16[32,1536]{1,0:T(8,128)(2,1)S(1)}, bf16[32,1536]{1,0:T(8,128)(2,1)S(1)}, u32[]{:S(2)}, u32[]{:S(2)}) %collective-permute-start.8) | collective-permute-done | bytes 98336 | tf_op jit(solution)/shard_map/ppermute | solution.py:155
  45.5 2.6 %down_1.1 = (f32[8,2048]{1,0:T(8,128)S(1)}, bf16[8,2048]{1,0:T(8,128)(2,1)S(1)}, bf16[8,2048]{1,0:T(8,128)(2,1)S(1)}, bf16[8,2048]{1,0:T(8,128)(2,1)S(1)}) custom-call(f32[32,2048]{1,0:T(8,128)S(1)} %get-tuple-element.40.refs_2_.refs_0_, bf16[32,1536]{1,0:T(8,128)(2,1)S(1)} %hidden.3.refs_1_, bf16[32,1536]{1,0:T(8,128)(2,1)S(1)} %collective-permute-done.8.refs_2_, ...), custom_call_target="tpu_custom_call" | custom-call | flops 1000 | bytes 1000 | tf_op jit(solution)/shard_map/down_1/pallas_call | solution.py:57
  48.0 2.8 %collective-permute-start.9 = (bf16[8,2048]{1,0:T(8,128)(2,1)S(1)}, bf16[8,2048]{1,0:T(8,128)(2,1)S(1)}, u32[]{:S(2)}, u32[]{:S(2)}) collective-permute-start(bf16[8,2048]{1,0:T(8,128)(2,1)S(1)} %get-tuple-element.44), channel_id=1, source_target_pairs={{0,12},{4,0},{8,4},{12,8},{1,13},{5,1},{9,5},{13,9},{2,14},{6,2},{... | collective-permute-start | bytes 98312 | tf_op jit(solution)/shard_map/ppermute | solution.py:141
  50.9 1.1 %collective-permute-start.10 = (bf16[8,2048]{1,0:T(8,128)(2,1)S(1)}, bf16[8,2048]{1,0:T(8,128)(2,1)S(1)}, u32[]{:S(2)}, u32[]{:S(2)}) collective-permute-start(bf16[8,2048]{1,0:T(8,128)(2,1)S(1)} %get-tuple-element.45), channel_id=1, source_target_pairs={{0,8},{4,12},{8,0},{12,4},{1,9},{5,13},{9,1},{13,5},{2,10},{6,14},... | collective-permute-start | bytes 98312 | tf_op jit(solution)/shard_map/ppermute | solution.py:141
  52.0 0.0 collective-permute-start.11
  52.0 0.6 %collective-permute-done.9 = bf16[8,2048]{1,0:T(8,128)(2,1)S(1)} collective-permute-done((bf16[8,2048]{1,0:T(8,128)(2,1)S(1)}, bf16[8,2048]{1,0:T(8,128)(2,1)S(1)}, u32[]{:S(2)}, u32[]{:S(2)}) %collective-permute-start.9) | collective-permute-done | bytes 32800 | tf_op jit(solution)/shard_map/ppermute | solution.py:141
  52.6 3.1 %collective-permute-done.10 = bf16[8,2048]{1,0:T(8,128)(2,1)S(1)} collective-permute-done((bf16[8,2048]{1,0:T(8,128)(2,1)S(1)}, bf16[8,2048]{1,0:T(8,128)(2,1)S(1)}, u32[]{:S(2)}, u32[]{:S(2)}) %collective-permute-start.10) | collective-permute-done | bytes 32800 | tf_op jit(solution)/shard_map/ppermute | solution.py:141
  55.7 2.0 %collective-permute-done.11 = bf16[8,2048]{1,0:T(8,128)(2,1)S(1)} collective-permute-done((bf16[8,2048]{1,0:T(8,128)(2,1)S(1)}, bf16[8,2048]{1,0:T(8,128)(2,1)S(1)}, u32[]{:S(2)}, u32[]{:S(2)}) %collective-permute-start.11) | collective-permute-done | bytes 32800 | tf_op jit(solution)/shard_map/ppermute | solution.py:141
  57.7 0.6 %add_convert_fusion = bf16[8,2048]{1,0:T(8,128)(2,1)} fusion(bf16[8,2048]{1,0:T(8,128)(2,1)S(1)} %collective-permute-done.11, bf16[8,2048]{1,0:T(8,128)(2,1)S(1)} %collective-permute-done.10, f32[8,2048]{1,0:T(8,128)S(1)} %get-tuple-element.43, bf16[8,2048]{1,0:T(8,128)(2,1)S(1)} %collective-permute-done.9), kind=kLoop, calls=%fused_computation.2 | loop fusion | flops 114688 | bytes 196608 | tf_op jit(solution)/shard_map/convert_element_type | solution.py:219
  (5 shorter events, 0.1 us)
Async XLA Ops:
  0.0 0.8 %copy-start = (bf16[8,2048]{1,0:T(8,128)(2,1)S(1)}, bf16[8,2048]{1,0:T(8,128)(2,1)}, u32[]{:S(2)}) copy-start(bf16[8,2048]{1,0:T(8,128)(2,1)} %refs_0_.3) | copy-start | bytes 98308
  4.0 11.7 %collective-permute-start.2 = (bf16[8,2048]{1,0:T(8,128)(2,1)S(1)}, bf16[8,2048]{1,0:T(8,128)(2,1)S(1)}, u32[]{:S(2)}, u32[]{:S(2)}) collective-permute-start(bf16[8,2048]{1,0:T(8,128)(2,1)S(1)} %get-tuple-element.26), channel_id=1, source_target_pairs={{0,12},{4,0},{8,4},{12,8},{1,13},{5,1},{9,5},{13,9},{2,14},{6,2},{... | collective-permute-start | bytes 98312 | tf_op jit(solution)/shard_map/ppermute | solution.py:141
  9.1 6.5 %collective-permute-start.1 = (bf16[8,2048]{1,0:T(8,128)(2,1)S(1)}, bf16[8,2048]{1,0:T(8,128)(2,1)S(1)}, u32[]{:S(2)}, u32[]{:S(2)}) collective-permute-start(bf16[8,2048]{1,0:T(8,128)(2,1)S(1)} %get-tuple-element.26), channel_id=1, source_target_pairs={{0,8},{4,12},{8,0},{12,4},{1,9},{5,13},{9,1},{13,5},{2,10},{6,14},... | collective-permute-start | bytes 98312 | tf_op jit(solution)/shard_map/ppermute | solution.py:141
  9.1 6.5 %collective-permute-start = (bf16[8,2048]{1,0:T(8,128)(2,1)S(1)}, bf16[8,2048]{1,0:T(8,128)(2,1)S(1)}, u32[]{:S(2)}, u32[]{:S(2)}) collective-permute-start(bf16[8,2048]{1,0:T(8,128)(2,1)S(1)} %get-tuple-element.26), channel_id=1, source_target_pairs={{0,4},{4,8},{8,12},{12,0},{1,5},{5,9},{9,13},{13,1},{2,6},{6,10},{... | collective-permute-start | bytes 98312 | tf_op jit(solution)/shard_map/ppermute | solution.py:141
  18.9 5.0 %collective-permute-start.3 = (bf16[32,3584]{1,0:T(8,128)(2,1)S(1)}, bf16[32,3584]{1,0:T(8,128)(2,1)S(1)}, u32[]{:S(2)}, u32[]{:S(2)}) collective-permute-start(bf16[32,3584]{1,0:T(8,128)(2,1)S(1)} %get-tuple-element.32), channel_id=1, source_target_pairs={{0,1},{1,0},{2,3},{3,2},{4,5},{5,4},{6,7},{7,6},{8,9},{9,8},{10,11... | collective-permute-start | bytes 688136 | tf_op jit(solution)/shard_map/ppermute | solution.py:155
  28.7 5.2 %collective-permute-start.5 = (bf16[32,3072]{1,0:T(8,128)(2,1)S(1)}, bf16[32,3072]{1,0:T(8,128)(2,1)S(1)}, u32[]{:S(2)}, u32[]{:S(2)}) collective-permute-start(bf16[32,3072]{1,0:T(8,128)(2,1)S(1)} %get-tuple-element.38), channel_id=1, source_target_pairs={{0,1},{1,0},{2,3},{3,2},{4,5},{5,4},{6,7},{7,6},{8,9},{9,8},{10,11... | collective-permute-start | bytes 589832 | tf_op jit(solution)/shard_map/ppermute | solution.py:155
  29.2 8.5 %collective-permute-start.4 = (bf16[32,3584]{1,0:T(8,128)(2,1)S(1)}, bf16[32,3584]{1,0:T(8,128)(2,1)S(1)}, u32[]{:S(2)}, u32[]{:S(2)}) collective-permute-start(bf16[32,3584]{1,0:T(8,128)(2,1)S(1)} %get-tuple-element.49.refs_5_), channel_id=1, source_target_pairs={{0,2},{1,3},{2,0},{3,1},{4,6},{5,7},{6,4},{7,5},{8,10},{9,11},{10,... | collective-permute-start | bytes 688136 | tf_op jit(solution)/shard_map/ppermute | solution.py:158
  34.0 10.0 %collective-permute-start.7 = (bf16[32,3072]{1,0:T(8,128)(2,1)S(1)}, bf16[32,3072]{1,0:T(8,128)(2,1)S(1)}, u32[]{:S(2)}, u32[]{:S(2)}) collective-permute-start(bf16[32,3072]{1,0:T(8,128)(2,1)S(1)} %get-tuple-element.47.refs_1_), channel_id=1, source_target_pairs={{0,2},{1,3},{2,0},{3,1},{4,6},{5,7},{6,4},{7,5},{8,10},{9,11},{10,... | collective-permute-start | bytes 589832 | tf_op jit(solution)/shard_map/ppermute | solution.py:158
  37.9 1.4 %collective-permute-start.6 = (bf16[32,1792]{1,0:T(8,128)(2,1)S(1)}, bf16[32,1792]{1,0:T(8,128)(2,1)S(1)}, u32[]{:S(2)}, u32[]{:S(2)}) collective-permute-start(bf16[32,1792]{1,0:T(8,128)(2,1)S(1)} %hidden.2.refs_0_), channel_id=1, source_target_pairs={{0,1},{1,0},{2,3},{3,2},{4,5},{5,4},{6,7},{7,6},{8,9},{9,8},{10,11... | collective-permute-start | bytes 344072 | tf_op jit(solution)/shard_map/ppermute | solution.py:155
  44.1 1.4 %collective-permute-start.8 = (bf16[32,1536]{1,0:T(8,128)(2,1)S(1)}, bf16[32,1536]{1,0:T(8,128)(2,1)S(1)}, u32[]{:S(2)}, u32[]{:S(2)}) collective-permute-start(bf16[32,1536]{1,0:T(8,128)(2,1)S(1)} %hidden.3.refs_1_), channel_id=1, source_target_pairs={{0,1},{1,0},{2,3},{3,2},{4,5},{5,4},{6,7},{7,6},{8,9},{9,8},{10,11... | collective-permute-start | bytes 294920 | tf_op jit(solution)/shard_map/ppermute | solution.py:155
  48.0 4.6 %collective-permute-start.9 = (bf16[8,2048]{1,0:T(8,128)(2,1)S(1)}, bf16[8,2048]{1,0:T(8,128)(2,1)S(1)}, u32[]{:S(2)}, u32[]{:S(2)}) collective-permute-start(bf16[8,2048]{1,0:T(8,128)(2,1)S(1)} %get-tuple-element.44), channel_id=1, source_target_pairs={{0,12},{4,0},{8,4},{12,8},{1,13},{5,1},{9,5},{13,9},{2,14},{6,2},{... | collective-permute-start | bytes 98312 | tf_op jit(solution)/shard_map/ppermute | solution.py:141
  50.9 4.8 %collective-permute-start.10 = (bf16[8,2048]{1,0:T(8,128)(2,1)S(1)}, bf16[8,2048]{1,0:T(8,128)(2,1)S(1)}, u32[]{:S(2)}, u32[]{:S(2)}) collective-permute-start(bf16[8,2048]{1,0:T(8,128)(2,1)S(1)} %get-tuple-element.45), channel_id=1, source_target_pairs={{0,8},{4,12},{8,0},{12,4},{1,9},{5,13},{9,1},{13,5},{2,10},{6,14},... | collective-permute-start | bytes 98312 | tf_op jit(solution)/shard_map/ppermute | solution.py:141
  52.0 5.7 %collective-permute-start.11 = (bf16[8,2048]{1,0:T(8,128)(2,1)S(1)}, bf16[8,2048]{1,0:T(8,128)(2,1)S(1)}, u32[]{:S(2)}, u32[]{:S(2)}) collective-permute-start(bf16[8,2048]{1,0:T(8,128)(2,1)S(1)} %get-tuple-element.46), channel_id=1, source_target_pairs={{0,4},{4,8},{8,12},{12,0},{1,5},{5,9},{9,13},{13,1},{2,6},{6,10},{... | collective-permute-start | bytes 98312 | tf_op jit(solution)/shard_map/ppermute | solution.py:141

commit v3 on v2

--- a/solution.py
+++ b/solution.py
@@ -105,8 +105,20 @@
     each_tile(w_own.shape[1], size, one)
 
 
+def sum_body(refs, out_refs):
+    keep_ref, got_ref = refs
+    total = keep_ref[...] + got_ref[...].astype(F32)
+    out_refs[0][...] = total
+    out_refs[1][...] = total.astype(BF16)
+
+
 def copy_body(refs, out_refs):
     out_refs[0][...] = refs[0][...]
+
+
+def join_body(refs, out_refs):
+    both = [ref[...].astype(F32) for ref in refs]
+    out_refs[0][...] = jnp.concatenate(both, axis=0).astype(BF16)
 
 
 def hidden_body(refs, out_refs):
@@ -137,19 +149,18 @@
     first = (half // 256 + 1) // 2 * 256
     chunks = [(0, first), (first, half - first)]
 
-    def shift(array, k):
-        return lax.ppermute(array, "ffn", [(i, (i + k) % n_ffn) for i in range(n_ffn)])
+    def start_of(chunk, mine):
+        return lambda core: (core if mine else 1 - core) * half + chunks[chunk][0]
 
     def wide(weight, chunk, mine):
-        at, width = chunks[chunk]
-        return weight, depth, width, lambda core: (0, (core if mine else 1 - core) * half + at), 4
+        return weight, depth, chunks[chunk][1], lambda core: (0, start_of(chunk, mine)(core)), 4
 
     def tall(chunk, mine):
-        at, height = chunks[chunk]
-        return down_weight, height, columns, lambda core: ((core if mine else 1 - core) * half + at, 0), 4
-
-    def sums(chunk, dtype):
-        return (rows, 2 * chunks[chunk][1]), dtype
+        return down_weight, chunks[chunk][1], columns, lambda core: (start_of(chunk, mine)(core), 0), 4
+
+    def gate_up(name, chunk, mine, blocks, fetches, deps=()):
+        shape = (rows, 2 * chunks[chunk][1])
+        return step(name, gate_up_body, [x, *blocks], [(shape, F32 if mine else BF16)], fetches, deps)
 
     def core_swap(array):
         return lax.ppermute(array, "mp", flip(n_mp, 1))
@@ -157,54 +168,41 @@
     def cross(array):
         return lax.ppermute(array, "mp", flip(n_mp, 2))
 
-    def hidden_of(total, crossed, dep):
+    def sum_of(keep, got, deps=()):
+        return step("sum", sum_body, [keep, got], [(keep.shape, F32), (keep.shape, BF16)], [], deps)
+
+    def hidden_of(total, crossed, deps=()):
         shape = (rows, total.shape[1] // 2)
-        return step("hidden", hidden_body, [total, crossed], [(shape, BF16)], [], [dep])[0]
-
-    tokens, g1s = step(
-        "fetch_0", copy_body, [tokens], [(tokens.shape, BF16)], [wide(gate_weight, 0, False)]
-    )
-    gathered = [tokens] + [shift(tokens, k) for k in range(1, n_ffn)]
-    u1s, g1k = step(
-        "fetch_1", None, [], [], [wide(up_weight, 0, False), wide(gate_weight, 0, True)], [g1s]
-    )
-    x = jnp.concatenate(gathered, axis=0)
-    send1, u1k = step("send_0", gate_up_body, [x, g1s, u1s], [sums(0, BF16)], [wide(up_weight, 0, True)])
+        return step("hidden", hidden_body, [total, crossed], [(shape, BF16)], [], deps)[0]
+
+    def join(array, other, dep):
+        shape = (2 * array.shape[0], depth)
+        return step("join", join_body, [array, other], [(shape, BF16)], [], [dep])[0]
+
+    gate, up = gate_weight, up_weight
+    other = lax.ppermute(tokens, "ffn", flip(n_ffn, 2))
+    (g1s,) = step("fetch_0", None, [], [], [wide(gate, 0, False)])
+    x = join(tokens, other, g1s)
+    other = lax.ppermute(x, "ffn", flip(n_ffn, 1))
+    u1s, g1k = step("fetch_1", None, [], [], [wide(up, 0, False), wide(gate, 0, True)], [x])
+    x = join(x, other, g1k)
+    send1, u1k = gate_up("send_0", 0, False, [g1s, u1s], [wide(up, 0, True)])
     got1 = core_swap(send1)
-    keep1, g2s, u2s = step(
-        "keep_0",
-        gate_up_body,
-        [x, g1k, u1k],
-        [sums(0, F32)],
-        [wide(gate_weight, 1, False), wide(up_weight, 1, False)],
-    )
-    sum1 = keep1 + got1.astype(F32)
-    out1 = sum1.astype(BF16)
+    keep1, g2s, u2s = gate_up("keep_0", 0, True, [g1k, u1k], [wide(gate, 1, False), wide(up, 1, False)], [send1])
+    sum1, out1 = sum_of(keep1, got1)
     crossed1 = cross(out1)
-    send2, g2k, u2k = step(
-        "send_1",
-        gate_up_body,
-        [x, g2s, u2s],
-        [sums(1, BF16)],
-        [wide(gate_weight, 1, True), wide(up_weight, 1, True)],
-        [out1],
-    )
+    send2, g2k, u2k = gate_up("send_1", 1, False, [g2s, u2s], [wide(gate, 1, True), wide(up, 1, True)], [out1])
     got2 = core_swap(send2)
-    keep2, d1k = step("keep_1", gate_up_body, [x, g2k, u2k], [sums(1, F32)], [tall(0, True)])
-    sum2 = keep2 + got2.astype(F32)
-    out2 = sum2.astype(BF16)
+    keep2, d1k = gate_up("keep_1", 1, True, [g2k, u2k], [tall(0, True)], [send2])
+    h1 = hidden_of(sum1, crossed1, [keep2])
+    sum2, out2 = sum_of(keep2, got2, [h1])
     crossed2 = cross(out2)
-    (d1s,) = step("fetch_down", None, [], [], [tall(0, False)], [out2])
-    h1 = hidden_of(sum1, crossed1, d1s)
     h1_other = core_swap(h1)
-    so_far, d2k, d2s = step(
-        "down_0",
-        down_body,
-        [h1, h1_other, d1k, d1s],
-        [((rows, columns), F32)],
-        [tall(1, True), tall(1, False)],
-    )
-    h2 = hidden_of(sum2, crossed2, so_far)
+    d1s, d2k = step("fetch_down", None, [], [], [tall(0, False), tall(1, True)], [out2])
+    so_far, d2s = step(
+        "down_0", down_body, [h1, h1_other, d1k, d1s], [((rows, columns), F32)], [tall(1, False)]
+    )
+    h2 = hidden_of(sum2, crossed2, [so_far])
     h2_other = core_swap(h2)
     part = (tokens.shape[0], columns)
     own, *sends = step(
@@ -214,8 +212,8 @@
         [(part, F32)] + [(part, BF16)] * (n_ffn - 1),
         [],
     )
-    for k, send in enumerate(sends, 1):
-        own = own + shift(send, n_ffn - k).astype(F32)
+    for bits, send in zip((2, 1, 3), sends):
+        own = own + lax.ppermute(send, "ffn", flip(n_ffn, bits)).astype(F32)
     return own.astype(BF16)
 
 
@@ -223,7 +221,7 @@
     n_ffn, n_mp = mesh.shape["ffn"], mesh.shape["mp"]
 
     def per_device(tokens, gate_weight, up_weight, down_weight):
-        fits = n_mp == 4 and n_ffn <= 4 and gate_weight.shape[1] % 1024 == 512
+        fits = n_mp == 4 and n_ffn == 4 and gate_weight.shape[1] % 1024 == 512
         if fits and tokens.shape[0] == 8:
             return ringed(n_ffn, n_mp, tokens, gate_weight, up_weight, down_weight)
         return plain(tokens, gate_weight, up_weight, down_weight)

time: 58.5 us -> 54.3 us (0.928)
  waiting for transfers between devices: 8.19 us -> 4.55 us
  local copies, waits for them, and re-layouts: 0.77 us -> 0.01 us
    ppermute x6 -> x5, waiting for transfers between devices: 5.72 us -> 3.6 us  [the longest x3 3.59 us: ringed(): own = own + lax.ppermute(send, 'ffn', flip(n_ffn, bits)).astype(F32)]
    ppermute x4, waiting for transfers between devices: 2.47 us -> 0.95 us  [core_swap(): return lax.ppermute(array, 'mp', flip(n_mp, 1))]
    unnamed x5 -> x2, local copies, waits for them, and re-layouts: 0.77 us -> 0.01 us
    pallas_call x11 -> x15, Pallas kernels: 35.4 us -> 35.6 us  [step(): pl.pallas_call(kernel, out_shape=out_shape, in_specs=[VMEM] * n_in + [ANY...]
    ppermute x6 -> x5, starting transfers between devices: 10.1 us -> 10.1 us  [the longest x3 4.42 us: ringed(): own = own + lax.ppermute(send, 'ffn', flip(n_ffn, bits)).astype(F32)]
  transfers between devices with their start and end apart: 12 -> 11, of which waited for: 5 -> 4; matrix products, arithmetic and copies ran while one was open for 0% -> 0% of each run, Pallas kernels for 37% -> 55%
where the time goes in v3:
time: 54.3 us; the launch traced here: 54.2 us
  Pallas kernels  35.6 us (66%)
  starting transfers between devices  13.2 us (24%)
  waiting for transfers between devices  4.55 us (8%)
  other arithmetic  0.63 us (1%)
    pallas_call x15, Pallas kernels, step(): pl.pallas_call(kernel, out_shape=out_shape, in_specs=[VMEM] * n_in + [ANY...  35.6 us
    ppermute x3, starting transfers between devices, ringed(): own = own + lax.ppermute(send, 'ffn', flip(n_ffn, bits)).astype(F32)  4.42 us
    ppermute x1, starting transfers between devices, ringed(): other = lax.ppermute(tokens, 'ffn', flip(n_ffn, 2))  4.04 us
    ppermute x3, waiting for transfers between devices, ringed(): own = own + lax.ppermute(send, 'ffn', flip(n_ffn, bits)).astype(F32)  3.59 us
    ppermute x2, starting transfers between devices, cross(): return lax.ppermute(array, 'mp', flip(n_mp, 2))  2.16 us
    ppermute x1, starting transfers between devices, ringed(): other = lax.ppermute(x, 'ffn', flip(n_ffn, 1))  1.64 us
  transfers between devices with their start and end apart: 11, of which 4 were waited for; matrix products, arithmetic and copies ran while one was open for 0% of the time, Pallas kernels for 55%

profile of v3, /device:TPU:0, one launch (start us, length us, event | category | flops | bytes accessed | tf_op | source)
XLA Modules:
  0.0 54.2 jit_solution(3604517004934051453)
XLA Ops:
  0.0 0.0 copy-start
  0.0 4.0 %collective-permute-start = (bf16[8,2048]{1,0:T(8,128)(2,1)}, bf16[8,2048]{1,0:T(8,128)(2,1)S(1)}, u32[]{:S(2)}, u32[]{:S(2)}) collective-permute-start(bf16[8,2048]{1,0:T(8,128)(2,1)} %refs_0_.5), channel_id=1, source_target_pairs={{0,8},{4,12},{8,0},{12,4},{1,9},{5,13},{9,1},{13,5},{2,10},{6,14},... | collective-permute-start | bytes 98312 | tf_op jit(solution)/shard_map/ppermute | solution.py:183
  4.0 3.2 %fetch_0.1.refs_2_.refs_1_ = bf16[2048,1792]{1,0:T(8,128)(2,1)S(1)} custom-call(bf16[2048,6656]{1,0:T(8,128)(2,1)} %refs_3_.6), custom_call_target="tpu_custom_call" | custom-call | flops 1000 | bytes 1000 | tf_op jit(solution)/shard_map/fetch_0/pallas_call | solution.py:57
  7.2 0.0 collective-permute-done.refs_1_
  7.3 0.0 copy-done
  7.3 1.6 %collective-permute-start.1 = (bf16[16,2048]{1,0:T(8,128)(2,1)S(1)}, bf16[16,2048]{1,0:T(8,128)(2,1)S(1)}, u32[]{:S(2)}, u32[]{:S(2)}) collective-permute-start(bf16[16,2048]{1,0:T(8,128)(2,1)S(1)} %join.2.refs_2_.refs_0_), channel_id=1, source_target_pairs={{0,4},{4,0},{8,12},{12,8},{1,5},{5,1},{9,13},{13,9},{2,6},{6,2},{1... | collective-permute-start | bytes 196616 | tf_op jit(solution)/shard_map/ppermute | solution.py:186
  8.9 5.5 %fetch_1.1 = (bf16[2048,1792]{1,0:T(8,128)(2,1)S(1)}, bf16[2048,1792]{1,0:T(8,128)(2,1)S(1)}) custom-call(bf16[2048,6656]{1,0:T(8,128)(2,1)} %refs_4_.4, bf16[2048,6656]{1,0:T(8,128)(2,1)} %refs_3_.6, bf16[16,2048]{1,0:T(8,128)(2,1)S(1)} %join.2.refs_2_.refs_0_), custom_call_target="tpu_custom_call" | custom-call | flops 1000 | bytes 1000 | tf_op jit(solution)/shard_map/fetch_1/pallas_call | solution.py:57
  14.4 0.0 collective-permute-done.1.refs_1_
  14.4 3.2 %send_0.1 = (bf16[32,3584]{1,0:T(8,128)(2,1)S(1)}, bf16[2048,1792]{1,0:T(8,128)(2,1)S(1)}) custom-call(bf16[32,2048]{1,0:T(8,128)(2,1)S(1)} %join.3.refs_0_, bf16[2048,1792]{1,0:T(8,128)(2,1)S(1)} %fetch_0.1.refs_2_.refs_1_, bf16[2048,1792]{1,0:T(8,128)(2,1)S(1)} %get-tuple-element.30.refs_2_, bf16[2048,6656]{1,0:T(8,128)(2,1)} %refs_4_.4), custom_call_target="tpu_custom_call" | custom-call | flops 1000 | bytes 1000 | tf_op jit(solution)/shard_map/send_0/pallas_call | solution.py:57
  17.7 0.1 collective-permute-start.2
  17.7 4.9 %keep_0.1 = (f32[32,3584]{1,0:T(8,128)S(1)}, bf16[2048,1536]{1,0:T(8,128)(2,1)S(1)}, bf16[2048,1536]{1,0:T(8,128)(2,1)S(1)}) custom-call(bf16[32,2048]{1,0:T(8,128)(2,1)S(1)} %join.3.refs_0_, bf16[2048,1792]{1,0:T(8,128)(2,1)S(1)} %get-tuple-element.29.refs_2_.refs_1_, bf16[2048,1792]{1,0:T(8,128)(2,1)S(1)} %get-tuple-element.31.refs_2_, ...), custom_call_target="tpu_custom_call" | custom-call | flops 1000 | bytes 1000 | tf_op jit(solution)/shard_map/keep_0/pallas_call | solution.py:57
  22.7 0.0 collective-permute-done.2.refs_1_
  22.7 0.1 sum.2
  22.7 1.6 %collective-permute-start.3 = (bf16[32,3584]{1,0:T(8,128)(2,1)S(1)}, bf16[32,3584]{1,0:T(8,128)(2,1)S(1)}, u32[]{:S(2)}, u32[]{:S(2)}) collective-permute-start(bf16[32,3584]{1,0:T(8,128)(2,1)S(1)} %get-tuple-element.35.refs_5_), channel_id=1, source_target_pairs={{0,2},{1,3},{2,0},{3,1},{4,6},{5,7},{6,4},{7,5},{8,10},{9,11},{10,... | collective-permute-start | bytes 688136 | tf_op jit(solution)/shard_map/ppermute | solution.py:169
  24.3 4.7 %send_1.1 = (bf16[32,3072]{1,0:T(8,128)(2,1)S(1)}, bf16[2048,1536]{1,0:T(8,128)(2,1)S(1)}, bf16[2048,1536]{1,0:T(8,128)(2,1)S(1)}) custom-call(bf16[32,2048]{1,0:T(8,128)(2,1)S(1)} %join.3.refs_0_, bf16[2048,1536]{1,0:T(8,128)(2,1)S(1)} %get-tuple-element.36.refs_1_, bf16[2048,1536]{1,0:T(8,128)(2,1)S(1)} %get-tuple-element.37.refs_2_, ...), custom_call_target="tpu_custom_call" | custom-call | flops 1000 | bytes 1000 | tf_op jit(solution)/shard_map/send_1/pallas_call | solution.py:57
  29.0 0.3 collective-permute-start.5
  29.3 3.2 %keep_1.1 = (f32[32,3072]{1,0:T(8,128)S(1)}, bf16[1792,2048]{1,0:T(8,128)(2,1)S(1)}) custom-call(bf16[32,2048]{1,0:T(8,128)(2,1)S(1)} %join.3.refs_0_, bf16[2048,1536]{1,0:T(8,128)(2,1)S(1)} %get-tuple-element.38.refs_1_, bf16[2048,1536]{1,0:T(8,128)(2,1)S(1)} %get-tuple-element.39.refs_2_, bf16[6656,2048]{1,0:T(8,128)(2,1)} %refs_4_.5, ...), custom_call_target="tpu_custom_call" | custom-call | flops 1000 | bytes 1000 | tf_op jit(solution)/shard_map/keep_1/pallas_call | solution.py:57
  32.5 0.0 collective-permute-done.3.refs_1_
  32.5 0.1 hidden.2.refs_2_.refs_0_
  32.6 0.0 collective-permute-done.5.refs_1_
  32.6 0.1 sum.3
  32.7 0.6 %collective-permute-start.6 = (bf16[32,3072]{1,0:T(8,128)(2,1)S(1)}, bf16[32,3072]{1,0:T(8,128)(2,1)S(1)}, u32[]{:S(2)}, u32[]{:S(2)}) collective-permute-start(bf16[32,3072]{1,0:T(8,128)(2,1)S(1)} %get-tuple-element.43.refs_2_), channel_id=1, source_target_pairs={{0,2},{1,3},{2,0},{3,1},{4,6},{5,7},{6,4},{7,5},{8,10},{9,11},{10,... | collective-permute-start | bytes 589832 | tf_op jit(solution)/shard_map/ppermute | solution.py:169
  33.3 0.0 collective-permute-start.4
  33.3 5.0 %fetch_down.1 = (bf16[1792,2048]{1,0:T(8,128)(2,1)S(1)}, bf16[1536,2048]{1,0:T(8,128)(2,1)S(1)}) custom-call(bf16[6656,2048]{1,0:T(8,128)(2,1)} %refs_4_.5, bf16[6656,2048]{1,0:T(8,128)(2,1)} %refs_4_.5, bf16[32,3072]{1,0:T(8,128)(2,1)S(1)} %get-tuple-element.43.refs_2_), custom_call_target="tpu_custom_call" | custom-call | flops 1000 | bytes 1000 | tf_op jit(solution)/shard_map/fetch_down/pallas_call | solution.py:57
  38.3 0.0 collective-permute-done.4.refs_1_
  38.3 3.0 %down_0.1 = (f32[32,2048]{1,0:T(8,128)S(1)}, bf16[1536,2048]{1,0:T(8,128)(2,1)S(1)}) custom-call(bf16[32,1792]{1,0:T(8,128)(2,1)S(1)} %hidden.2.refs_2_.refs_0_, bf16[32,1792]{1,0:T(8,128)(2,1)S(1)} %collective-permute-done.4.refs_1_, bf16[1792,2048]{1,0:T(8,128)(2,1)S(1)} %get-tuple-element.42.refs_2_, bf16[1792,2048]{1,0:T(8,128)(2,1)S(1)} %get-tuple-element.44.refs_3_, ...), custom_call_target="tpu_custom_call" | custom-call | flops 1000 | bytes 1000 | tf_op jit(solution)/shard_map/down_0/pallas_call | solution.py:57
  41.4 0.0 collective-permute-done.6.refs_1_
  41.4 0.1 hidden.3.refs_1_
  41.5 0.5 %collective-permute-start.7 = (bf16[32,1536]{1,0:T(8,128)(2,1)S(1)}, bf16[32,1536]{1,0:T(8,128)(2,1)S(1)}, u32[]{:S(2)}, u32[]{:S(2)}) collective-permute-start(bf16[32,1536]{1,0:T(8,128)(2,1)S(1)} %hidden.3.refs_1_), channel_id=1, source_target_pairs={{0,1},{1,0},{2,3},{3,2},{4,5},{5,4},{6,7},{7,6},{8,9},{9,8},{10,11... | collective-permute-start | bytes 294920 | tf_op jit(solution)/shard_map/ppermute | solution.py:166
  42.0 0.9 %collective-permute-done.7.refs_2_ = bf16[32,1536]{1,0:T(8,128)(2,1)S(1)} collective-permute-done((bf16[32,1536]{1,0:T(8,128)(2,1)S(1)}, bf16[32,1536]{1,0:T(8,128)(2,1)S(1)}, u32[]{:S(2)}, u32[]{:S(2)}) %collective-permute-start.7) | collective-permute-done | bytes 98336 | tf_op jit(solution)/shard_map/ppermute | solution.py:166
  43.0 2.6 %down_1.1 = (f32[8,2048]{1,0:T(8,128)S(1)}, bf16[8,2048]{1,0:T(8,128)(2,1)S(1)}, bf16[8,2048]{1,0:T(8,128)(2,1)S(1)}, bf16[8,2048]{1,0:T(8,128)(2,1)S(1)}) custom-call(f32[32,2048]{1,0:T(8,128)S(1)} %get-tuple-element.45.refs_2_.refs_0_, bf16[32,1536]{1,0:T(8,128)(2,1)S(1)} %hidden.3.refs_1_, bf16[32,1536]{1,0:T(8,128)(2,1)S(1)} %collective-permute-done.7.refs_2_, ...), custom_call_target="tpu_custom_call" | custom-call | flops 1000 | bytes 1000 | tf_op jit(solution)/shard_map/down_1/pallas_call | solution.py:57
  45.5 2.1 %collective-permute-start.8 = (bf16[8,2048]{1,0:T(8,128)(2,1)S(1)}, bf16[8,2048]{1,0:T(8,128)(2,1)S(1)}, u32[]{:S(2)}, u32[]{:S(2)}) collective-permute-start(bf16[8,2048]{1,0:T(8,128)(2,1)S(1)} %get-tuple-element.50), channel_id=1, source_target_pairs={{0,8},{4,12},{8,0},{12,4},{1,9},{5,13},{9,1},{13,5},{2,10},{6,14},... | collective-permute-start | bytes 98312 | tf_op jit(solution)/shard_map/ppermute | solution.py:216
  47.6 0.2 collective-permute-start.9
  47.8 2.1 %collective-permute-start.10 = (bf16[8,2048]{1,0:T(8,128)(2,1)S(1)}, bf16[8,2048]{1,0:T(8,128)(2,1)S(1)}, u32[]{:S(2)}, u32[]{:S(2)}) collective-permute-start(bf16[8,2048]{1,0:T(8,128)(2,1)S(1)} %get-tuple-element.52), channel_id=1, source_target_pairs={{0,12},{4,8},{8,4},{12,0},{1,13},{5,9},{9,5},{13,1},{2,14},{6,10},... | collective-permute-start | bytes 98312 | tf_op jit(solution)/shard_map/ppermute | solution.py:216
  49.9 0.8 %collective-permute-done.8 = bf16[8,2048]{1,0:T(8,128)(2,1)S(1)} collective-permute-done((bf16[8,2048]{1,0:T(8,128)(2,1)S(1)}, bf16[8,2048]{1,0:T(8,128)(2,1)S(1)}, u32[]{:S(2)}, u32[]{:S(2)}) %collective-permute-start.8) | collective-permute-done | bytes 32800 | tf_op jit(solution)/shard_map/ppermute | solution.py:216
  50.8 0.7 %collective-permute-done.9 = bf16[8,2048]{1,0:T(8,128)(2,1)S(1)} collective-permute-done((bf16[8,2048]{1,0:T(8,128)(2,1)S(1)}, bf16[8,2048]{1,0:T(8,128)(2,1)S(1)}, u32[]{:S(2)}, u32[]{:S(2)}) %collective-permute-start.9) | collective-permute-done | bytes 32800 | tf_op jit(solution)/shard_map/ppermute | solution.py:216
  51.5 2.0 %collective-permute-done.10 = bf16[8,2048]{1,0:T(8,128)(2,1)S(1)} collective-permute-done((bf16[8,2048]{1,0:T(8,128)(2,1)S(1)}, bf16[8,2048]{1,0:T(8,128)(2,1)S(1)}, u32[]{:S(2)}, u32[]{:S(2)}) %collective-permute-start.10) | collective-permute-done | bytes 32800 | tf_op jit(solution)/shard_map/ppermute | solution.py:216
  53.5 0.6 %add_convert_fusion = bf16[8,2048]{1,0:T(8,128)(2,1)} fusion(bf16[8,2048]{1,0:T(8,128)(2,1)S(1)} %collective-permute-done.10, bf16[8,2048]{1,0:T(8,128)(2,1)S(1)} %collective-permute-done.9, f32[8,2048]{1,0:T(8,128)S(1)} %get-tuple-element.49, bf16[8,2048]{1,0:T(8,128)(2,1)S(1)} %collective-permute-done.8), kind=kLoop, calls=%fused_computation | loop fusion | flops 114688 | bytes 196608 | tf_op jit(solution)/shard_map/convert_element_type | solution.py:217
  (2 shorter events, 0.0 us)
Async XLA Ops:
  0.0 7.3 %copy-start = (bf16[8,2048]{1,0:T(8,128)(2,1)S(1)}, bf16[8,2048]{1,0:T(8,128)(2,1)}, u32[]{:S(2)}) copy-start(bf16[8,2048]{1,0:T(8,128)(2,1)} %refs_0_.5) | copy-start | bytes 98308
  0.0 7.2 %collective-permute-start = (bf16[8,2048]{1,0:T(8,128)(2,1)}, bf16[8,2048]{1,0:T(8,128)(2,1)S(1)}, u32[]{:S(2)}, u32[]{:S(2)}) collective-permute-start(bf16[8,2048]{1,0:T(8,128)(2,1)} %refs_0_.5), channel_id=1, source_target_pairs={{0,8},{4,12},{8,0},{12,4},{1,9},{5,13},{9,1},{13,5},{2,10},{6,14},... | collective-permute-start | bytes 98312 | tf_op jit(solution)/shard_map/ppermute | solution.py:183
  7.3 7.1 %collective-permute-start.1 = (bf16[16,2048]{1,0:T(8,128)(2,1)S(1)}, bf16[16,2048]{1,0:T(8,128)(2,1)S(1)}, u32[]{:S(2)}, u32[]{:S(2)}) collective-permute-start(bf16[16,2048]{1,0:T(8,128)(2,1)S(1)} %join.2.refs_2_.refs_0_), channel_id=1, source_target_pairs={{0,4},{4,0},{8,12},{12,8},{1,5},{5,1},{9,13},{13,9},{2,6},{6,2},{1... | collective-permute-start | bytes 196616 | tf_op jit(solution)/shard_map/ppermute | solution.py:186
  17.7 5.0 %collective-permute-start.2 = (bf16[32,3584]{1,0:T(8,128)(2,1)S(1)}, bf16[32,3584]{1,0:T(8,128)(2,1)S(1)}, u32[]{:S(2)}, u32[]{:S(2)}) collective-permute-start(bf16[32,3584]{1,0:T(8,128)(2,1)S(1)} %get-tuple-element.32.refs_5_), channel_id=1, source_target_pairs={{0,1},{1,0},{2,3},{3,2},{4,5},{5,4},{6,7},{7,6},{8,9},{9,8},{10,11... | collective-permute-start | bytes 688136 | tf_op jit(solution)/shard_map/ppermute | solution.py:166
  22.7 9.8 %collective-permute-start.3 = (bf16[32,3584]{1,0:T(8,128)(2,1)S(1)}, bf16[32,3584]{1,0:T(8,128)(2,1)S(1)}, u32[]{:S(2)}, u32[]{:S(2)}) collective-permute-start(bf16[32,3584]{1,0:T(8,128)(2,1)S(1)} %get-tuple-element.35.refs_5_), channel_id=1, source_target_pairs={{0,2},{1,3},{2,0},{3,1},{4,6},{5,7},{6,4},{7,5},{8,10},{9,11},{10,... | collective-permute-start | bytes 688136 | tf_op jit(solution)/shard_map/ppermute | solution.py:169
  29.0 3.6 %collective-permute-start.5 = (bf16[32,3072]{1,0:T(8,128)(2,1)S(1)}, bf16[32,3072]{1,0:T(8,128)(2,1)S(1)}, u32[]{:S(2)}, u32[]{:S(2)}) collective-permute-start(bf16[32,3072]{1,0:T(8,128)(2,1)S(1)} %get-tuple-element.40.refs_4_), channel_id=1, source_target_pairs={{0,1},{1,0},{2,3},{3,2},{4,5},{5,4},{6,7},{7,6},{8,9},{9,8},{10,11... | collective-permute-start | bytes 589832 | tf_op jit(solution)/shard_map/ppermute | solution.py:166
  32.7 8.7 %collective-permute-start.6 = (bf16[32,3072]{1,0:T(8,128)(2,1)S(1)}, bf16[32,3072]{1,0:T(8,128)(2,1)S(1)}, u32[]{:S(2)}, u32[]{:S(2)}) collective-permute-start(bf16[32,3072]{1,0:T(8,128)(2,1)S(1)} %get-tuple-element.43.refs_2_), channel_id=1, source_target_pairs={{0,2},{1,3},{2,0},{3,1},{4,6},{5,7},{6,4},{7,5},{8,10},{9,11},{10,... | collective-permute-start | bytes 589832 | tf_op jit(solution)/shard_map/ppermute | solution.py:169
  33.3 5.0 %collective-permute-start.4 = (bf16[32,1792]{1,0:T(8,128)(2,1)S(1)}, bf16[32,1792]{1,0:T(8,128)(2,1)S(1)}, u32[]{:S(2)}, u32[]{:S(2)}) collective-permute-start(bf16[32,1792]{1,0:T(8,128)(2,1)S(1)} %hidden.2.refs_2_.refs_0_), channel_id=1, source_target_pairs={{0,1},{1,0},{2,3},{3,2},{4,5},{5,4},{6,7},{7,6},{8,9},{9,8},{10,11... | collective-permute-start | bytes 344072 | tf_op jit(solution)/shard_map/ppermute | solution.py:166
  41.5 1.5 %collective-permute-start.7 = (bf16[32,1536]{1,0:T(8,128)(2,1)S(1)}, bf16[32,1536]{1,0:T(8,128)(2,1)S(1)}, u32[]{:S(2)}, u32[]{:S(2)}) collective-permute-start(bf16[32,1536]{1,0:T(8,128)(2,1)S(1)} %hidden.3.refs_1_), channel_id=1, source_target_pairs={{0,1},{1,0},{2,3},{3,2},{4,5},{5,4},{6,7},{7,6},{8,9},{9,8},{10,11... | collective-permute-start | bytes 294920 | tf_op jit(solution)/shard_map/ppermute | solution.py:166
  45.5 5.3 %collective-permute-start.8 = (bf16[8,2048]{1,0:T(8,128)(2,1)S(1)}, bf16[8,2048]{1,0:T(8,128)(2,1)S(1)}, u32[]{:S(2)}, u32[]{:S(2)}) collective-permute-start(bf16[8,2048]{1,0:T(8,128)(2,1)S(1)} %get-tuple-element.50), channel_id=1, source_target_pairs={{0,8},{4,12},{8,0},{12,4},{1,9},{5,13},{9,1},{13,5},{2,10},{6,14},... | collective-permute-start | bytes 98312 | tf_op jit(solution)/shard_map/ppermute | solution.py:216
  47.6 3.9 %collective-permute-start.9 = (bf16[8,2048]{1,0:T(8,128)(2,1)S(1)}, bf16[8,2048]{1,0:T(8,128)(2,1)S(1)}, u32[]{:S(2)}, u32[]{:S(2)}) collective-permute-start(bf16[8,2048]{1,0:T(8,128)(2,1)S(1)} %get-tuple-element.51), channel_id=1, source_target_pairs={{0,4},{4,0},{8,12},{12,8},{1,5},{5,1},{9,13},{13,9},{2,6},{6,2},{1... | collective-permute-start | bytes 98312 | tf_op jit(solution)/shard_map/ppermute | solution.py:216
  47.8 5.7 %collective-permute-start.10 = (bf16[8,2048]{1,0:T(8,128)(2,1)S(1)}, bf16[8,2048]{1,0:T(8,128)(2,1)S(1)}, u32[]{:S(2)}, u32[]{:S(2)}) collective-permute-start(bf16[8,2048]{1,0:T(8,128)(2,1)S(1)} %get-tuple-element.52), channel_id=1, source_target_pairs={{0,12},{4,8},{8,4},{12,0},{1,13},{5,9},{9,5},{13,1},{2,14},{6,10},... | collective-permute-start | bytes 98312 | tf_op jit(solution)/shard_map/ppermute | solution.py:216

commit v4 on v3

--- a/solution.py
+++ b/solution.py
@@ -66,7 +66,7 @@
     )(*ins, *(in_hbm(weight) for weight, *_ in fetches), *deps)
 
 
-def tiled(width, most=1024):
+def tiled(width, most=768):
     return max(t for t in range(128, most + 1, 128) if width % t == 0)
 
 
@@ -146,17 +146,17 @@
     depth, columns = gate_weight.shape[0], down_weight.shape[1]
     rows = tokens.shape[0] * n_ffn
     half = gate_weight.shape[1] // 2
-    first = (half // 256 + 1) // 2 * 256
+    first = half // 256 * 9 // 13 * 256
     chunks = [(0, first), (first, half - first)]
 
     def start_of(chunk, mine):
         return lambda core: (core if mine else 1 - core) * half + chunks[chunk][0]
 
     def wide(weight, chunk, mine):
-        return weight, depth, chunks[chunk][1], lambda core: (0, start_of(chunk, mine)(core)), 4
+        return weight, depth, chunks[chunk][1], lambda core: (0, start_of(chunk, mine)(core)), 1
 
     def tall(chunk, mine):
-        return down_weight, chunks[chunk][1], columns, lambda core: (start_of(chunk, mine)(core), 0), 4
+        return down_weight, chunks[chunk][1], columns, lambda core: (start_of(chunk, mine)(core), 0), 1
 
     def gate_up(name, chunk, mine, blocks, fetches, deps=()):
         shape = (rows, 2 * chunks[chunk][1])
@@ -198,12 +198,17 @@
     sum2, out2 = sum_of(keep2, got2, [h1])
     crossed2 = cross(out2)
     h1_other = core_swap(h1)
-    d1s, d2k = step("fetch_down", None, [], [], [tall(0, False), tall(1, True)], [out2])
-    so_far, d2s = step(
-        "down_0", down_body, [h1, h1_other, d1k, d1s], [((rows, columns), F32)], [tall(1, False)]
-    )
-    h2 = hidden_of(sum2, crossed2, [so_far])
+    (d1s,) = step("fetch_down", None, [], [], [tall(0, False)], [out2])
+    h2 = hidden_of(sum2, crossed2, [d1s])
     h2_other = core_swap(h2)
+    so_far, d2k, d2s = step(
+        "down_0",
+        down_body,
+        [h1, h1_other, d1k, d1s],
+        [((rows, columns), F32)],
+        [tall(1, True), tall(1, False)],
+        [h2],
+    )
     part = (tokens.shape[0], columns)
     own, *sends = step(
         "down_1",

time: 54.3 us -> 53.6 us (0.987)
  waiting for transfers between devices: 4.55 us -> 3.59 us
  starting transfers between devices: 13.2 us -> 14 us
  Pallas kernels: 35.6 us -> 34.9 us
    ppermute x2, starting transfers between devices: 2.16 us -> 3.11 us  [cross(): return lax.ppermute(array, 'mp', flip(n_mp, 2))]
    ppermute x4, waiting for transfers between devices: 0.95 us -> 0.01 us  [core_swap(): return lax.ppermute(array, 'mp', flip(n_mp, 1))]
    pallas_call x15, Pallas kernels: 35.6 us -> 34.9 us  [step(): pl.pallas_call(kernel, out_shape=out_shape, in_specs=[VMEM] * n_in + [ANY...]
    ppermute x3, waiting for transfers between devices: 3.59 us -> 3.03 us  [ringed(): own = own + lax.ppermute(send, 'ffn', flip(n_ffn, bits)).astype(F32)]
  transfers between devices with their start and end apart: 11 -> 11, of which waited for: 4 -> 5; matrix products, arithmetic and copies ran while one was open for 0% -> 0% of each run, Pallas kernels for 55% -> 54%
where the time goes in v4:
time: 53.6 us; the launch traced here: 53.3 us
  Pallas kernels  34.9 us (65%)
  starting transfers between devices  14 us (26%)
  waiting for transfers between devices  3.59 us (7%)
  other arithmetic  0.64 us (1%)
    pallas_call x15, Pallas kernels, step(): pl.pallas_call(kernel, out_shape=out_shape, in_specs=[VMEM] * n_in + [ANY...  34.9 us
    ppermute x3, starting transfers between devices, ringed(): own = own + lax.ppermute(send, 'ffn', flip(n_ffn, bits)).astype(F32)  4.4 us
    ppermute x1, starting transfers between devices, ringed(): other = lax.ppermute(tokens, 'ffn', flip(n_ffn, 2))  4.04 us
    ppermute x2, starting transfers between devices, cross(): return lax.ppermute(array, 'mp', flip(n_mp, 2))  3.11 us
    ppermute x3, waiting for transfers between devices, ringed(): own = own + lax.ppermute(send, 'ffn', flip(n_ffn, bits)).astype(F32)  3.03 us
    ppermute x1, starting transfers between devices, ringed(): other = lax.ppermute(x, 'ffn', flip(n_ffn, 1))  1.64 us
  transfers between devices with their start and end apart: 11, of which 5 were waited for; matrix products, arithmetic and copies ran while one was open for 0% of the time, Pallas kernels for 54%

profile of v4, /device:TPU:0, one launch (start us, length us, event | category | flops | bytes accessed | tf_op | source)
XLA Modules:
  0.0 53.3 jit_solution(1410457780436689410)
XLA Ops:
  0.0 0.0 copy-start
  0.0 4.0 %collective-permute-start = (bf16[8,2048]{1,0:T(8,128)(2,1)}, bf16[8,2048]{1,0:T(8,128)(2,1)S(1)}, u32[]{:S(2)}, u32[]{:S(2)}) collective-permute-start(bf16[8,2048]{1,0:T(8,128)(2,1)} %refs_0_.5), channel_id=1, source_target_pairs={{0,8},{4,12},{8,0},{12,4},{1,9},{5,13},{9,1},{13,5},{2,10},{6,14},... | collective-permute-start | bytes 98312 | tf_op jit(solution)/shard_map/ppermute | solution.py:183
  4.0 3.8 %fetch_0.1.refs_2_.refs_1_ = bf16[2048,2304]{1,0:T(8,128)(2,1)S(1)} custom-call(bf16[2048,6656]{1,0:T(8,128)(2,1)} %refs_3_.6), custom_call_target="tpu_custom_call" | custom-call | flops 1000 | bytes 1000 | tf_op jit(solution)/shard_map/fetch_0/pallas_call | solution.py:57
  7.8 0.0 collective-permute-done.refs_1_
  7.8 0.0 copy-done
  7.8 1.6 %collective-permute-start.1 = (bf16[16,2048]{1,0:T(8,128)(2,1)S(1)}, bf16[16,2048]{1,0:T(8,128)(2,1)S(1)}, u32[]{:S(2)}, u32[]{:S(2)}) collective-permute-start(bf16[16,2048]{1,0:T(8,128)(2,1)S(1)} %join.2.refs_2_.refs_0_), channel_id=1, source_target_pairs={{0,4},{4,0},{8,12},{12,8},{1,5},{5,1},{9,13},{13,9},{2,6},{6,2},{1... | collective-permute-start | bytes 196616 | tf_op jit(solution)/shard_map/ppermute | solution.py:186
  9.5 6.5 %fetch_1.1 = (bf16[2048,2304]{1,0:T(8,128)(2,1)S(1)}, bf16[2048,2304]{1,0:T(8,128)(2,1)S(1)}) custom-call(bf16[2048,6656]{1,0:T(8,128)(2,1)} %refs_4_.4, bf16[2048,6656]{1,0:T(8,128)(2,1)} %refs_3_.6, bf16[16,2048]{1,0:T(8,128)(2,1)S(1)} %join.2.refs_2_.refs_0_), custom_call_target="tpu_custom_call" | custom-call | flops 1000 | bytes 1000 | tf_op jit(solution)/shard_map/fetch_1/pallas_call | solution.py:57
  16.0 0.0 collective-permute-done.1.refs_1_
  16.0 3.9 %send_0.1 = (bf16[32,4608]{1,0:T(8,128)(2,1)S(1)}, bf16[2048,2304]{1,0:T(8,128)(2,1)S(1)}) custom-call(bf16[32,2048]{1,0:T(8,128)(2,1)S(1)} %join.3.refs_0_, bf16[2048,2304]{1,0:T(8,128)(2,1)S(1)} %fetch_0.1.refs_2_.refs_1_, bf16[2048,2304]{1,0:T(8,128)(2,1)S(1)} %get-tuple-element.29.refs_2_, bf16[2048,6656]{1,0:T(8,128)(2,1)} %refs_4_.4), custom_call_target="tpu_custom_call" | custom-call | flops 1000 | bytes 1000 | tf_op jit(solution)/shard_map/send_0/pallas_call | solution.py:57
  20.0 0.1 collective-permute-start.2
  20.1 3.9 %keep_0.1 = (f32[32,4608]{1,0:T(8,128)S(1)}, bf16[2048,1024]{1,0:T(8,128)(2,1)S(1)}, bf16[2048,1024]{1,0:T(8,128)(2,1)S(1)}) custom-call(bf16[32,2048]{1,0:T(8,128)(2,1)S(1)} %join.3.refs_0_, bf16[2048,2304]{1,0:T(8,128)(2,1)S(1)} %get-tuple-element.28.refs_2_.refs_1_, bf16[2048,2304]{1,0:T(8,128)(2,1)S(1)} %get-tuple-element.30.refs_2_, ...), custom_call_target="tpu_custom_call" | custom-call | flops 1000 | bytes 1000 | tf_op jit(solution)/shard_map/keep_0/pallas_call | solution.py:57
  24.0 0.0 collective-permute-done.2.refs_1_
  24.0 0.1 sum.2
  24.1 1.6 %collective-permute-start.3 = (bf16[32,4608]{1,0:T(8,128)(2,1)S(1)}, bf16[32,4608]{1,0:T(8,128)(2,1)S(1)}, u32[]{:S(2)}, u32[]{:S(2)}) collective-permute-start(bf16[32,4608]{1,0:T(8,128)(2,1)S(1)} %get-tuple-element.34.refs_5_), channel_id=1, source_target_pairs={{0,2},{1,3},{2,0},{3,1},{4,6},{5,7},{6,4},{7,5},{8,10},{9,11},{10,... | collective-permute-start | bytes 884744 | tf_op jit(solution)/shard_map/ppermute | solution.py:169
  25.6 3.5 %send_1.1 = (bf16[32,2048]{1,0:T(8,128)(2,1)S(1)}, bf16[2048,1024]{1,0:T(8,128)(2,1)S(1)}, bf16[2048,1024]{1,0:T(8,128)(2,1)S(1)}) custom-call(bf16[32,2048]{1,0:T(8,128)(2,1)S(1)} %join.3.refs_0_, bf16[2048,1024]{1,0:T(8,128)(2,1)S(1)} %get-tuple-element.35.refs_1_, bf16[2048,1024]{1,0:T(8,128)(2,1)S(1)} %get-tuple-element.36.refs_2_, ...), custom_call_target="tpu_custom_call" | custom-call | flops 1000 | bytes 1000 | tf_op jit(solution)/shard_map/send_1/pallas_call | solution.py:57
  29.1 0.3 collective-permute-start.5
  29.4 3.7 %keep_1.1 = (f32[32,2048]{1,0:T(8,128)S(1)}, bf16[2304,2048]{1,0:T(8,128)(2,1)S(1)}) custom-call(bf16[32,2048]{1,0:T(8,128)(2,1)S(1)} %join.3.refs_0_, bf16[2048,1024]{1,0:T(8,128)(2,1)S(1)} %get-tuple-element.37.refs_1_, bf16[2048,1024]{1,0:T(8,128)(2,1)S(1)} %get-tuple-element.38.refs_2_, bf16[6656,2048]{1,0:T(8,128)(2,1)} %refs_5_.1, ...), custom_call_target="tpu_custom_call" | custom-call | flops 1000 | bytes 1000 | tf_op jit(solution)/shard_map/keep_1/pallas_call | solution.py:57
  33.1 0.4 collective-permute-done.3.refs_1_
  33.6 0.1 hidden.2.refs_2_.refs_0_
  33.7 0.0 collective-permute-done.5.refs_1_
  33.7 1.6 %collective-permute-start.6 = (bf16[32,2048]{1,0:T(8,128)(2,1)S(1)}, bf16[32,2048]{1,0:T(8,128)(2,1)S(1)}, u32[]{:S(2)}, u32[]{:S(2)}) collective-permute-start(bf16[32,2048]{1,0:T(8,128)(2,1)S(1)} %get-tuple-element.42.refs_1_), channel_id=1, source_target_pairs={{0,2},{1,3},{2,0},{3,1},{4,6},{5,7},{6,4},{7,5},{8,10},{9,11},{10,... | collective-permute-start | bytes 393224 | tf_op jit(solution)/shard_map/ppermute | solution.py:169
  35.3 0.0 collective-permute-start.4
  35.3 3.7 %fetch_down.1.refs_2_.refs_3_ = bf16[2304,2048]{1,0:T(8,128)(2,1)S(1)} custom-call(bf16[6656,2048]{1,0:T(8,128)(2,1)} %refs_5_.1, bf16[32,2048]{1,0:T(8,128)(2,1)S(1)} %get-tuple-element.42.refs_1_), custom_call_target="tpu_custom_call" | custom-call | flops 1000 | bytes 1000 | tf_op jit(solution)/shard_map/fetch_down/pallas_call | solution.py:57
  39.0 0.1 collective-permute-done.6.refs_1_
  39.1 0.1 hidden.3.refs_6_.refs_1_
  39.1 0.5 collective-permute-start.7
  39.6 0.0 collective-permute-done.4.refs_1_
  39.6 3.7 %down_0.1 = (f32[32,2048]{1,0:T(8,128)S(1)}, bf16[1024,2048]{1,0:T(8,128)(2,1)S(1)}, bf16[1024,2048]{1,0:T(8,128)(2,1)S(1)}) custom-call(bf16[32,2304]{1,0:T(8,128)(2,1)S(1)} %hidden.2.refs_2_.refs_0_, bf16[32,2304]{1,0:T(8,128)(2,1)S(1)} %collective-permute-done.4.refs_1_, bf16[2304,2048]{1,0:T(8,128)(2,1)S(1)} %get-tuple-element.41.refs_2_, ...), custom_call_target="tpu_custom_call" | custom-call | flops 1000 | bytes 1000 | tf_op jit(solution)/shard_map/down_0/pallas_call | solution.py:57
  43.4 0.0 collective-permute-done.7.refs_2_
  43.4 1.9 %down_1.1 = (f32[8,2048]{1,0:T(8,128)S(1)}, bf16[8,2048]{1,0:T(8,128)(2,1)S(1)}, bf16[8,2048]{1,0:T(8,128)(2,1)S(1)}, bf16[8,2048]{1,0:T(8,128)(2,1)S(1)}) custom-call(f32[32,2048]{1,0:T(8,128)S(1)} %get-tuple-element.44.refs_0_, bf16[32,1024]{1,0:T(8,128)(2,1)S(1)} %hidden.3.refs_6_.refs_1_, bf16[32,1024]{1,0:T(8,128)(2,1)S(1)} %collective-permute-done.7.refs_2_, ...), custom_call_target="tpu_custom_call" | custom-call | flops 1000 | bytes 1000 | tf_op jit(solution)/shard_map/down_1/pallas_call | solution.py:57
  45.3 1.5 %collective-permute-start.8 = (bf16[8,2048]{1,0:T(8,128)(2,1)S(1)}, bf16[8,2048]{1,0:T(8,128)(2,1)S(1)}, u32[]{:S(2)}, u32[]{:S(2)}) collective-permute-start(bf16[8,2048]{1,0:T(8,128)(2,1)S(1)} %get-tuple-element.48), channel_id=1, source_target_pairs={{0,8},{4,12},{8,0},{12,4},{1,9},{5,13},{9,1},{13,5},{2,10},{6,14},... | collective-permute-start | bytes 98312 | tf_op jit(solution)/shard_map/ppermute | solution.py:221
  46.8 0.2 collective-permute-start.9
  47.0 2.7 %collective-permute-start.10 = (bf16[8,2048]{1,0:T(8,128)(2,1)S(1)}, bf16[8,2048]{1,0:T(8,128)(2,1)S(1)}, u32[]{:S(2)}, u32[]{:S(2)}) collective-permute-start(bf16[8,2048]{1,0:T(8,128)(2,1)S(1)} %get-tuple-element.50), channel_id=1, source_target_pairs={{0,12},{4,8},{8,4},{12,0},{1,13},{5,9},{9,5},{13,1},{2,14},{6,10},... | collective-permute-start | bytes 98312 | tf_op jit(solution)/shard_map/ppermute | solution.py:221
  49.7 0.7 %collective-permute-done.8 = bf16[8,2048]{1,0:T(8,128)(2,1)S(1)} collective-permute-done((bf16[8,2048]{1,0:T(8,128)(2,1)S(1)}, bf16[8,2048]{1,0:T(8,128)(2,1)S(1)}, u32[]{:S(2)}, u32[]{:S(2)}) %collective-permute-start.8) | collective-permute-done | bytes 32800 | tf_op jit(solution)/shard_map/ppermute | solution.py:221
  50.3 0.4 collective-permute-done.9
  50.7 2.0 %collective-permute-done.10 = bf16[8,2048]{1,0:T(8,128)(2,1)S(1)} collective-permute-done((bf16[8,2048]{1,0:T(8,128)(2,1)S(1)}, bf16[8,2048]{1,0:T(8,128)(2,1)S(1)}, u32[]{:S(2)}, u32[]{:S(2)}) %collective-permute-start.10) | collective-permute-done | bytes 32800 | tf_op jit(solution)/shard_map/ppermute | solution.py:221
  52.7 0.6 %add_convert_fusion = bf16[8,2048]{1,0:T(8,128)(2,1)} fusion(bf16[8,2048]{1,0:T(8,128)(2,1)S(1)} %collective-permute-done.10, bf16[8,2048]{1,0:T(8,128)(2,1)S(1)} %collective-permute-done.9, f32[8,2048]{1,0:T(8,128)S(1)} %get-tuple-element.47, bf16[8,2048]{1,0:T(8,128)(2,1)S(1)} %collective-permute-done.8), kind=kLoop, calls=%fused_computation | loop fusion | flops 114688 | bytes 196608 | tf_op jit(solution)/shard_map/convert_element_type | solution.py:222
  (3 shorter events, 0.1 us)
Async XLA Ops:
  0.0 7.8 %copy-start = (bf16[8,2048]{1,0:T(8,128)(2,1)S(1)}, bf16[8,2048]{1,0:T(8,128)(2,1)}, u32[]{:S(2)}) copy-start(bf16[8,2048]{1,0:T(8,128)(2,1)} %refs_0_.5) | copy-start | bytes 98308
  0.0 7.8 %collective-permute-start = (bf16[8,2048]{1,0:T(8,128)(2,1)}, bf16[8,2048]{1,0:T(8,128)(2,1)S(1)}, u32[]{:S(2)}, u32[]{:S(2)}) collective-permute-start(bf16[8,2048]{1,0:T(8,128)(2,1)} %refs_0_.5), channel_id=1, source_target_pairs={{0,8},{4,12},{8,0},{12,4},{1,9},{5,13},{9,1},{13,5},{2,10},{6,14},... | collective-permute-start | bytes 98312 | tf_op jit(solution)/shard_map/ppermute | solution.py:183
  7.8 8.2 %collective-permute-start.1 = (bf16[16,2048]{1,0:T(8,128)(2,1)S(1)}, bf16[16,2048]{1,0:T(8,128)(2,1)S(1)}, u32[]{:S(2)}, u32[]{:S(2)}) collective-permute-start(bf16[16,2048]{1,0:T(8,128)(2,1)S(1)} %join.2.refs_2_.refs_0_), channel_id=1, source_target_pairs={{0,4},{4,0},{8,12},{12,8},{1,5},{5,1},{9,13},{13,9},{2,6},{6,2},{1... | collective-permute-start | bytes 196616 | tf_op jit(solution)/shard_map/ppermute | solution.py:186
  20.0 4.0 %collective-permute-start.2 = (bf16[32,4608]{1,0:T(8,128)(2,1)S(1)}, bf16[32,4608]{1,0:T(8,128)(2,1)S(1)}, u32[]{:S(2)}, u32[]{:S(2)}) collective-permute-start(bf16[32,4608]{1,0:T(8,128)(2,1)S(1)} %get-tuple-element.31.refs_5_), channel_id=1, source_target_pairs={{0,1},{1,0},{2,3},{3,2},{4,5},{5,4},{6,7},{7,6},{8,9},{9,8},{10,11... | collective-permute-start | bytes 884744 | tf_op jit(solution)/shard_map/ppermute | solution.py:166
  24.1 9.5 %collective-permute-start.3 = (bf16[32,4608]{1,0:T(8,128)(2,1)S(1)}, bf16[32,4608]{1,0:T(8,128)(2,1)S(1)}, u32[]{:S(2)}, u32[]{:S(2)}) collective-permute-start(bf16[32,4608]{1,0:T(8,128)(2,1)S(1)} %get-tuple-element.34.refs_5_), channel_id=1, source_target_pairs={{0,2},{1,3},{2,0},{3,1},{4,6},{5,7},{6,4},{7,5},{8,10},{9,11},{10,... | collective-permute-start | bytes 884744 | tf_op jit(solution)/shard_map/ppermute | solution.py:169
  29.1 4.5 %collective-permute-start.5 = (bf16[32,2048]{1,0:T(8,128)(2,1)S(1)}, bf16[32,2048]{1,0:T(8,128)(2,1)S(1)}, u32[]{:S(2)}, u32[]{:S(2)}) collective-permute-start(bf16[32,2048]{1,0:T(8,128)(2,1)S(1)} %get-tuple-element.39.refs_4_), channel_id=1, source_target_pairs={{0,1},{1,0},{2,3},{3,2},{4,5},{5,4},{6,7},{7,6},{8,9},{9,8},{10,11... | collective-permute-start | bytes 393224 | tf_op jit(solution)/shard_map/ppermute | solution.py:166
  33.7 5.4 %collective-permute-start.6 = (bf16[32,2048]{1,0:T(8,128)(2,1)S(1)}, bf16[32,2048]{1,0:T(8,128)(2,1)S(1)}, u32[]{:S(2)}, u32[]{:S(2)}) collective-permute-start(bf16[32,2048]{1,0:T(8,128)(2,1)S(1)} %get-tuple-element.42.refs_1_), channel_id=1, source_target_pairs={{0,2},{1,3},{2,0},{3,1},{4,6},{5,7},{6,4},{7,5},{8,10},{9,11},{10,... | collective-permute-start | bytes 393224 | tf_op jit(solution)/shard_map/ppermute | solution.py:169
  35.3 4.4 %collective-permute-start.4 = (bf16[32,2304]{1,0:T(8,128)(2,1)S(1)}, bf16[32,2304]{1,0:T(8,128)(2,1)S(1)}, u32[]{:S(2)}, u32[]{:S(2)}) collective-permute-start(bf16[32,2304]{1,0:T(8,128)(2,1)S(1)} %hidden.2.refs_2_.refs_0_), channel_id=1, source_target_pairs={{0,1},{1,0},{2,3},{3,2},{4,5},{5,4},{6,7},{7,6},{8,9},{9,8},{10,11... | collective-permute-start | bytes 442376 | tf_op jit(solution)/shard_map/ppermute | solution.py:166
  39.1 4.2 %collective-permute-start.7 = (bf16[32,1024]{1,0:T(8,128)(2,1)S(1)}, bf16[32,1024]{1,0:T(8,128)(2,1)S(1)}, u32[]{:S(2)}, u32[]{:S(2)}) collective-permute-start(bf16[32,1024]{1,0:T(8,128)(2,1)S(1)} %hidden.3.refs_6_.refs_1_), channel_id=1, source_target_pairs={{0,1},{1,0},{2,3},{3,2},{4,5},{5,4},{6,7},{7,6},{8,9},{9,8},{10,11... | collective-permute-start | bytes 196616 | tf_op jit(solution)/shard_map/ppermute | solution.py:166
  45.3 5.1 %collective-permute-start.8 = (bf16[8,2048]{1,0:T(8,128)(2,1)S(1)}, bf16[8,2048]{1,0:T(8,128)(2,1)S(1)}, u32[]{:S(2)}, u32[]{:S(2)}) collective-permute-start(bf16[8,2048]{1,0:T(8,128)(2,1)S(1)} %get-tuple-element.48), channel_id=1, source_target_pairs={{0,8},{4,12},{8,0},{12,4},{1,9},{5,13},{9,1},{13,5},{2,10},{6,14},... | collective-permute-start | bytes 98312 | tf_op jit(solution)/shard_map/ppermute | solution.py:221
  46.8 3.9 %collective-permute-start.9 = (bf16[8,2048]{1,0:T(8,128)(2,1)S(1)}, bf16[8,2048]{1,0:T(8,128)(2,1)S(1)}, u32[]{:S(2)}, u32[]{:S(2)}) collective-permute-start(bf16[8,2048]{1,0:T(8,128)(2,1)S(1)} %get-tuple-element.49), channel_id=1, source_target_pairs={{0,4},{4,0},{8,12},{12,8},{1,5},{5,1},{9,13},{13,9},{2,6},{6,2},{1... | collective-permute-start | bytes 98312 | tf_op jit(solution)/shard_map/ppermute | solution.py:221
  47.0 5.7 %collective-permute-start.10 = (bf16[8,2048]{1,0:T(8,128)(2,1)S(1)}, bf16[8,2048]{1,0:T(8,128)(2,1)S(1)}, u32[]{:S(2)}, u32[]{:S(2)}) collective-permute-start(bf16[8,2048]{1,0:T(8,128)(2,1)S(1)} %get-tuple-element.50), channel_id=1, source_target_pairs={{0,12},{4,8},{8,4},{12,0},{1,13},{5,9},{9,5},{13,1},{2,14},{6,10},... | collective-permute-start | bytes 98312 | tf_op jit(solution)/shard_map/ppermute | solution.py:221

commit v5 on v3

--- a/solution.py
+++ b/solution.py
@@ -66,7 +66,7 @@
     )(*ins, *(in_hbm(weight) for weight, *_ in fetches), *deps)
 
 
-def tiled(width, most=1024):
+def tiled(width, most=1152):
     return max(t for t in range(128, most + 1, 128) if width % t == 0)
 
 
@@ -142,31 +142,42 @@
     return total.astype(BF16)
 
 
-def ringed(n_ffn, n_mp, tokens, gate_weight, up_weight, down_weight):
+def shared(n_groups, n_ffn, n_mp, tokens, gate_weight, up_weight, down_weight):
     depth, columns = gate_weight.shape[0], down_weight.shape[1]
-    rows = tokens.shape[0] * n_ffn
-    half = gate_weight.shape[1] // 2
-    first = (half // 256 + 1) // 2 * 256
-    chunks = [(0, first), (first, half - first)]
-
-    def start_of(chunk, mine):
-        return lambda core: (core if mine else 1 - core) * half + chunks[chunk][0]
+    few = tokens.shape[0]
+    rows = few * n_ffn * n_groups
+    half = gate_weight.shape[1] // n_groups
+    quarter = half // 2
+    first = quarter // 128 * 9 // 13 * 128
+    chunks = [(0, first), (first, quarter - first)]
+
+    def swap(array, axis, size, bit):
+        return lax.ppermute(array, axis, flip(size, bit))
+
+    def start_of(chunk, mine, core):
+        owner = core if mine else 1 - core
+        return lax.axis_index("groups") * half + owner * quarter + chunks[chunk][0]
 
     def wide(weight, chunk, mine):
-        return weight, depth, chunks[chunk][1], lambda core: (0, start_of(chunk, mine)(core)), 4
-
-    def tall(chunk, mine):
-        return down_weight, chunks[chunk][1], columns, lambda core: (start_of(chunk, mine)(core), 0), 4
-
-    def gate_up(name, chunk, mine, blocks, fetches, deps=()):
-        shape = (rows, 2 * chunks[chunk][1])
-        return step(name, gate_up_body, [x, *blocks], [(shape, F32 if mine else BF16)], fetches, deps)
+        return weight, depth, chunks[chunk][1], lambda core: (0, start_of(chunk, mine, core)), 1
+
+    def both(chunk, mine):
+        return [wide(gate_weight, chunk, mine), wide(up_weight, chunk, mine)]
+
+    def tall(chunk):
+        return [
+            (down_weight, chunks[chunk][1], columns, lambda core, mine=mine: (start_of(chunk, mine, core), 0), 1)
+            for mine in (True, False)
+        ]
+
+    def sums(chunk, dtype):
+        return (rows, 2 * chunks[chunk][1]), dtype
 
     def core_swap(array):
-        return lax.ppermute(array, "mp", flip(n_mp, 1))
+        return swap(array, "mp", n_mp, 1)
 
     def cross(array):
-        return lax.ppermute(array, "mp", flip(n_mp, 2))
+        return swap(array, "mp", n_mp, 2)
 
     def sum_of(keep, got, deps=()):
         return step("sum", sum_body, [keep, got], [(keep.shape, F32), (keep.shape, BF16)], [], deps)
@@ -179,51 +190,51 @@
         shape = (2 * array.shape[0], depth)
         return step("join", join_body, [array, other], [(shape, BF16)], [], [dep])[0]
 
-    gate, up = gate_weight, up_weight
-    other = lax.ppermute(tokens, "ffn", flip(n_ffn, 2))
-    (g1s,) = step("fetch_0", None, [], [], [wide(gate, 0, False)])
+    other = swap(tokens, "ffn", n_ffn, 2)
+    g1s, u1s = step("fetch_0", None, [], [], both(0, False))
     x = join(tokens, other, g1s)
-    other = lax.ppermute(x, "ffn", flip(n_ffn, 1))
-    u1s, g1k = step("fetch_1", None, [], [], [wide(up, 0, False), wide(gate, 0, True)], [x])
+    other = swap(x, "ffn", n_ffn, 1)
+    g1k, u1k = step("fetch_1", None, [], [], both(0, True), [x])
     x = join(x, other, g1k)
-    send1, u1k = gate_up("send_0", 0, False, [g1s, u1s], [wide(up, 0, True)])
+    other = swap(x, "groups", n_groups, 1)
+    g2s, u2s, g2k, u2k = step("fetch_2", None, [], [], both(1, False) + both(1, True), [x])
+    x = join(x, other, g2s)
+    (send1,) = step("send_0", gate_up_body, [x, g1s, u1s], [sums(0, BF16)], [])
     got1 = core_swap(send1)
-    keep1, g2s, u2s = gate_up("keep_0", 0, True, [g1k, u1k], [wide(gate, 1, False), wide(up, 1, False)], [send1])
+    (keep1,) = step("keep_0", gate_up_body, [x, g1k, u1k], [sums(0, F32)], [], [send1])
     sum1, out1 = sum_of(keep1, got1)
     crossed1 = cross(out1)
-    send2, g2k, u2k = gate_up("send_1", 1, False, [g2s, u2s], [wide(gate, 1, True), wide(up, 1, True)], [out1])
+    (send2,) = step("send_1", gate_up_body, [x, g2s, u2s], [sums(1, BF16)], [], [out1])
     got2 = core_swap(send2)
-    keep2, d1k = gate_up("keep_1", 1, True, [g2k, u2k], [tall(0, True)], [send2])
-    h1 = hidden_of(sum1, crossed1, [keep2])
-    sum2, out2 = sum_of(keep2, got2, [h1])
+    (keep2,) = step("keep_1", gate_up_body, [x, g2k, u2k], [sums(1, F32)], [], [send2])
+    sum2, out2 = sum_of(keep2, got2)
     crossed2 = cross(out2)
+    d1k, d1s, d2k, d2s = step("fetch_3", None, [], [], tall(0) + tall(1), [out2])
+    h1 = hidden_of(sum1, crossed1, [d1k])
     h1_other = core_swap(h1)
-    d1s, d2k = step("fetch_down", None, [], [], [tall(0, False), tall(1, True)], [out2])
-    so_far, d2s = step(
-        "down_0", down_body, [h1, h1_other, d1k, d1s], [((rows, columns), F32)], [tall(1, False)]
+    h2 = hidden_of(sum2, crossed2, [h1])
+    h2_other = core_swap(h2)
+    (so_far,) = step("down_0", down_body, [h1, h1_other, d1k, d1s], [((rows, columns), F32)], [], [h2])
+    part = (rows // 2, columns)
+    own, send = step(
+        "down_1", down_body, [so_far, h2, h2_other, d2k, d2s], [(part, F32), (part, BF16)], []
     )
-    h2 = hidden_of(sum2, crossed2, [so_far])
-    h2_other = core_swap(h2)
-    part = (tokens.shape[0], columns)
-    own, *sends = step(
-        "down_1",
-        down_body,
-        [so_far, h2, h2_other, d2k, d2s],
-        [(part, F32)] + [(part, BF16)] * (n_ffn - 1),
-        [],
-    )
-    for bits, send in zip((2, 1, 3), sends):
-        own = own + lax.ppermute(send, "ffn", flip(n_ffn, bits)).astype(F32)
-    return own.astype(BF16)
+    own = own + swap(send, "groups", n_groups, 1).astype(F32)
+    few = tokens.shape[0]
+    total = own[:few]
+    for k, bits in ((1, 2), (2, 1), (3, 3)):
+        send = own[k * few : (k + 1) * few].astype(BF16)
+        total = total + swap(send, "ffn", n_ffn, bits).astype(F32)
+    return total.astype(BF16)
 
 
 def solution(mesh):
-    n_ffn, n_mp = mesh.shape["ffn"], mesh.shape["mp"]
+    n_groups, n_ffn, n_mp = mesh.shape["groups"], mesh.shape["ffn"], mesh.shape["mp"]
 
     def per_device(tokens, gate_weight, up_weight, down_weight):
-        fits = n_mp == 4 and n_ffn == 4 and gate_weight.shape[1] % 1024 == 512
+        fits = (n_groups, n_ffn, n_mp) == (2, 4, 4) and gate_weight.shape[1] % 512 == 0
         if fits and tokens.shape[0] == 8:
-            return ringed(n_ffn, n_mp, tokens, gate_weight, up_weight, down_weight)
+            return shared(n_groups, n_ffn, n_mp, tokens, gate_weight, up_weight, down_weight)
         return plain(tokens, gate_weight, up_weight, down_weight)
 
     in_specs = (P(("groups", "ffn"), "mp"), P("mp", "ffn"), P("mp", "ffn"), P("ffn", "mp"))

time: 54.3 us -> 52 us (0.958)
  Pallas kernels: 35.6 us -> 25 us
  waiting for transfers between devices: 4.55 us -> 11 us
  starting transfers between devices: 13.2 us -> 15 us
    pallas_call x15 -> x17, Pallas kernels: 35.6 us -> 25 us  [step(): pl.pallas_call(kernel, out_shape=out_shape, in_specs=[VMEM] * n_in + [ANY...]
    ppermute x11 -> x13, waiting for transfers between devices: 4.55 us -> 11 us  [swap(): return lax.ppermute(array, axis, flip(size, bit))]
    ppermute x11 -> x13, starting transfers between devices: 13.2 us -> 15 us  [swap(): return lax.ppermute(array, axis, flip(size, bit))]
  transfers between devices with their start and end apart: 11 -> 13, of which waited for: 4 -> 6; matrix products, arithmetic and copies ran while one was open for 0% -> 0% of each run, Pallas kernels for 55% -> 42%
where the time goes in v5:
time: 52 us; the launch traced here: 51.9 us
  Pallas kernels  25 us (48%)
  starting transfers between devices  15 us (29%)
  waiting for transfers between devices  11 us (21%)
  other arithmetic  0.66 us (1%)
    pallas_call x17, Pallas kernels, step(): pl.pallas_call(kernel, out_shape=out_shape, in_specs=[VMEM] * n_in + [ANY...  25 us
    ppermute x13, starting transfers between devices, swap(): return lax.ppermute(array, axis, flip(size, bit))  15 us
    ppermute x13, waiting for transfers between devices, swap(): return lax.ppermute(array, axis, flip(size, bit))  11 us
  transfers between devices with their start and end apart: 13, of which 6 were waited for; matrix products, arithmetic and copies ran while one was open for 0% of the time, Pallas kernels for 42%

profile of v5, /device:TPU:0, one launch (start us, length us, event | category | flops | bytes accessed | tf_op | source)
XLA Modules:
  0.0 51.9 jit_solution(2288291473271619477)
XLA Ops:
  0.0 0.0 copy-start
  0.0 4.0 %collective-permute-start = (bf16[8,2048]{1,0:T(8,128)(2,1)}, bf16[8,2048]{1,0:T(8,128)(2,1)S(1)}, u32[]{:S(2)}, u32[]{:S(2)}) collective-permute-start(bf16[8,2048]{1,0:T(8,128)(2,1)} %refs_0_.6), channel_id=1, source_target_pairs={{0,8},{4,12},{8,0},{12,4},{1,9},{5,13},{9,1},{13,5},{2,10},{6,14},... | collective-permute-start | bytes 98312 | tf_op jit(solution)/shard_map/ppermute | solution.py:155
  4.0 3.8 %fetch_0.1 = (bf16[2048,1152]{1,0:T(8,128)(2,1)S(1)}, bf16[2048,1152]{1,0:T(8,128)(2,1)S(1)}) custom-call(bf16[2048,6656]{1,0:T(8,128)(2,1)} %refs_2_.2, bf16[2048,6656]{1,0:T(8,128)(2,1)} %refs_3_.2), custom_call_target="tpu_custom_call" | custom-call | flops 1000 | bytes 1000 | tf_op jit(solution)/shard_map/fetch_0/pallas_call | solution.py:57
  7.9 0.0 collective-permute-done.refs_1_
  7.9 0.0 copy-done
  7.9 1.6 %collective-permute-start.1 = (bf16[16,2048]{1,0:T(8,128)(2,1)S(1)}, bf16[16,2048]{1,0:T(8,128)(2,1)S(1)}, u32[]{:S(2)}, u32[]{:S(2)}) collective-permute-start(bf16[16,2048]{1,0:T(8,128)(2,1)S(1)} %join.3.refs_2_.refs_0_), channel_id=1, source_target_pairs={{0,4},{4,0},{8,12},{12,8},{1,5},{5,1},{9,13},{13,9},{2,6},{6,2},{1... | collective-permute-start | bytes 196616 | tf_op jit(solution)/shard_map/ppermute | solution.py:155
  9.5 3.8 %fetch_1.1 = (bf16[2048,1152]{1,0:T(8,128)(2,1)S(1)}, bf16[2048,1152]{1,0:T(8,128)(2,1)S(1)}) custom-call(bf16[2048,6656]{1,0:T(8,128)(2,1)} %refs_2_.2, bf16[2048,6656]{1,0:T(8,128)(2,1)} %refs_3_.2, bf16[16,2048]{1,0:T(8,128)(2,1)S(1)} %join.3.refs_2_.refs_0_), custom_call_target="tpu_custom_call" | custom-call | flops 1000 | bytes 1000 | tf_op jit(solution)/shard_map/fetch_1/pallas_call | solution.py:57
  13.4 0.0 collective-permute-done.1.refs_1_
  13.4 1.6 %collective-permute-start.2 = (bf16[32,2048]{1,0:T(8,128)(2,1)S(1)}, bf16[32,2048]{1,0:T(8,128)(2,1)S(1)}, u32[]{:S(2)}, u32[]{:S(2)}) collective-permute-start(bf16[32,2048]{1,0:T(8,128)(2,1)S(1)} %join.4.refs_4_.refs_0_), channel_id=1, source_target_pairs={{0,16},{16,0},{1,17},{17,1},{2,18},{18,2},{3,19},{19,3},{4,20},{20... | collective-permute-start | bytes 393224 | tf_op jit(solution)/shard_map/ppermute | solution.py:155
  15.0 3.5 %fetch_2.1 = (bf16[2048,512]{1,0:T(8,128)(2,1)S(1)}, bf16[2048,512]{1,0:T(8,128)(2,1)S(1)}, bf16[2048,512]{1,0:T(8,128)(2,1)S(1)}, bf16[2048,512]{1,0:T(8,128)(2,1)S(1)}) custom-call(bf16[2048,6656]{1,0:T(8,128)(2,1)} %refs_2_.2, bf16[2048,6656]{1,0:T(8,128)(2,1)} %refs_3_.2, bf16[2048,6656]{1,0:T(8,128)(2,1)} %refs_2_.2, bf16[2048,6656]{1,0:T(8,128)(2,1)} %refs_3_.2, ...), custom_call_target="tpu_custom_call" | custom-call | flops 1000 | bytes 1000 | tf_op jit(solution)/shard_map/fetch_2/pallas_call | solution.py:57
  18.6 0.0 collective-permute-done.2.refs_1_
  18.6 1.7 %send_0.1.refs_3_ = bf16[64,2304]{1,0:T(8,128)(2,1)S(1)} custom-call(bf16[64,2048]{1,0:T(8,128)(2,1)S(1)} %join.5.refs_0_, bf16[2048,1152]{1,0:T(8,128)(2,1)S(1)} %get-tuple-element.23.refs_2_.refs_1_, bf16[2048,1152]{1,0:T(8,128)(2,1)S(1)} %get-tuple-element.27.refs_2_), custom_call_target="tpu_custom_call" | custom-call | flops 1000 | bytes 1000 | tf_op jit(solution)/shard_map/send_0/pallas_call | solution.py:57
  20.3 0.1 collective-permute-start.3
  20.4 1.7 %keep_0.1.refs_0_ = f32[64,2304]{1,0:T(8,128)S(1)} custom-call(bf16[64,2048]{1,0:T(8,128)(2,1)S(1)} %join.5.refs_0_, bf16[2048,1152]{1,0:T(8,128)(2,1)S(1)} %get-tuple-element.24.refs_2_.refs_1_, bf16[2048,1152]{1,0:T(8,128)(2,1)S(1)} %get-tuple-element.26.refs_2_, bf16[64,2304]{1,0:T(8,128)(2,1)S(1)} %send_0.1.refs_3_), custom_call_target="tpu_custom_call" | custom-call | flops 1000 | bytes 1000 | tf_op jit(solution)/shard_map/keep_0/pallas_call | solution.py:57
  22.2 0.0 collective-permute-done.3.refs_1_
  22.2 0.1 sum.2
  22.3 1.6 %collective-permute-start.4 = (bf16[64,2304]{1,0:T(8,128)(2,1)S(1)}, bf16[64,2304]{1,0:T(8,128)(2,1)S(1)}, u32[]{:S(2)}, u32[]{:S(2)}) collective-permute-start(bf16[64,2304]{1,0:T(8,128)(2,1)S(1)} %get-tuple-element.29.refs_3_), channel_id=1, source_target_pairs={{0,2},{1,3},{2,0},{3,1},{4,6},{5,7},{6,4},{7,5},{8,10},{9,11},{10,... | collective-permute-start | bytes 884744 | tf_op jit(solution)/shard_map/ppermute | solution.py:155
  23.8 0.8 %send_1.1.refs_3_ = bf16[64,1024]{1,0:T(8,128)(2,1)S(1)} custom-call(bf16[64,2048]{1,0:T(8,128)(2,1)S(1)} %join.5.refs_0_, bf16[2048,512]{1,0:T(8,128)(2,1)S(1)} %get-tuple-element.25.refs_2_.refs_1_, bf16[2048,512]{1,0:T(8,128)(2,1)S(1)} %get-tuple-element.32.refs_2_, bf16[64,2304]{1,0:T(8,128)(2,1)S(1)} %get-tuple-element.29.refs_3_), custom_call_target="tpu_custom_call" | custom-call | flops 1000 | bytes 1000 | tf_op jit(solution)/shard_map/send_1/pallas_call | solution.py:57
  24.7 0.3 collective-permute-start.5
  24.9 0.8 %keep_1.1.refs_0_ = f32[64,1024]{1,0:T(8,128)S(1)} custom-call(bf16[64,2048]{1,0:T(8,128)(2,1)S(1)} %join.5.refs_0_, bf16[2048,512]{1,0:T(8,128)(2,1)S(1)} %get-tuple-element.30.refs_1_, bf16[2048,512]{1,0:T(8,128)(2,1)S(1)} %get-tuple-element.31.refs_2_, bf16[64,1024]{1,0:T(8,128)(2,1)S(1)} %send_1.1.refs_3_), custom_call_target="tpu_custom_call" | custom-call | flops 1000 | bytes 1000 | tf_op jit(solution)/shard_map/keep_1/pallas_call | solution.py:57
  25.8 0.3 collective-permute-done.5.refs_1_
  26.1 0.6 %collective-permute-start.7 = (bf16[64,1024]{1,0:T(8,128)(2,1)S(1)}, bf16[64,1024]{1,0:T(8,128)(2,1)S(1)}, u32[]{:S(2)}, u32[]{:S(2)}) collective-permute-start(bf16[64,1024]{1,0:T(8,128)(2,1)S(1)} %get-tuple-element.33.refs_4_), channel_id=1, source_target_pairs={{0,2},{1,3},{2,0},{3,1},{4,6},{5,7},{6,4},{7,5},{8,10},{9,11},{10,... | collective-permute-start | bytes 393224 | tf_op jit(solution)/shard_map/ppermute | solution.py:155
  26.7 5.0 %fetch_3.1 = (bf16[1152,2048]{1,0:T(8,128)(2,1)S(1)}, bf16[1152,2048]{1,0:T(8,128)(2,1)S(1)}, bf16[512,2048]{1,0:T(8,128)(2,1)S(1)}, bf16[512,2048]{1,0:T(8,128)(2,1)S(1)}) custom-call(bf16[6656,2048]{1,0:T(8,128)(2,1)} %refs_3_.3, bf16[6656,2048]{1,0:T(8,128)(2,1)} %refs_3_.3, bf16[6656,2048]{1,0:T(8,128)(2,1)} %refs_3_.3, bf16[6656,2048]{1,0:T(8,128)(2,1)} %refs_3_.3, ...), custom_call_target="tpu_custom_call" | custom-call | flops 1000 | bytes 1000 | tf_op jit(solution)/shard_map/fetch_3/pallas_call | solution.py:57
  31.7 0.4 collective-permute-done.4.refs_1_
  32.1 0.1 hidden.2.refs_2_.refs_0_
  32.3 0.1 collective-permute-start.6
  32.3 2.2 %collective-permute-done.7.refs_1_ = bf16[64,1024]{1,0:T(8,128)(2,1)S(1)} collective-permute-done((bf16[64,1024]{1,0:T(8,128)(2,1)S(1)}, bf16[64,1024]{1,0:T(8,128)(2,1)S(1)}, u32[]{:S(2)}, u32[]{:S(2)}) %collective-permute-start.7) | collective-permute-done | bytes 131104 | tf_op jit(solution)/shard_map/ppermute | solution.py:155
  34.5 0.1 hidden.3.refs_4_.refs_1_
  34.6 0.1 collective-permute-start.8
  34.7 0.0 collective-permute-done.6.refs_1_
  34.7 2.1 %down_0.1.refs_0_ = f32[64,2048]{1,0:T(8,128)S(1)} custom-call(bf16[64,1152]{1,0:T(8,128)(2,1)S(1)} %hidden.2.refs_2_.refs_0_, bf16[64,1152]{1,0:T(8,128)(2,1)S(1)} %collective-permute-done.6.refs_1_, bf16[1152,2048]{1,0:T(8,128)(2,1)S(1)} %get-tuple-element.34.refs_2_, bf16[1152,2048]{1,0:T(8,128)(2,1)S(1)} %get-tuple-element.35.refs_3_, ...), custom_call_target="tpu_custom_call" | custom-call | flops 1000 | bytes 1000 | tf_op jit(solution)/shard_map/down_0/pallas_call | solution.py:57
  36.8 0.0 collective-permute-done.8.refs_2_
  36.9 1.2 %down_1.1 = (f32[32,2048]{1,0:T(8,128)S(1)}, bf16[32,2048]{1,0:T(8,128)(2,1)S(1)}) custom-call(f32[64,2048]{1,0:T(8,128)S(1)} %down_0.1.refs_0_, bf16[64,512]{1,0:T(8,128)(2,1)S(1)} %hidden.3.refs_4_.refs_1_, bf16[64,512]{1,0:T(8,128)(2,1)S(1)} %collective-permute-done.8.refs_2_, bf16[512,2048]{1,0:T(8,128)(2,1)S(1)} %get-tuple-element.37.refs_3_, ...), custom_call_target="tpu_custom_call" | custom-call | flops 1000 | bytes 1000 | tf_op jit(solution)/shard_map/down_1/pallas_call | solution.py:57
  38.1 1.5 %collective-permute-start.9 = (bf16[32,2048]{1,0:T(8,128)(2,1)S(1)}, bf16[32,2048]{1,0:T(8,128)(2,1)S(1)}, u32[]{:S(2)}, u32[]{:S(2)}) collective-permute-start(bf16[32,2048]{1,0:T(8,128)(2,1)S(1)} %get-tuple-element.40), channel_id=1, source_target_pairs={{0,16},{16,0},{1,17},{17,1},{2,18},{18,2},{3,19},{19,3},{4,20},{20... | collective-permute-start | bytes 393224 | tf_op jit(solution)/shard_map/ppermute | solution.py:155
  39.5 4.5 %collective-permute-done.9 = bf16[32,2048]{1,0:T(8,128)(2,1)S(1)} collective-permute-done((bf16[32,2048]{1,0:T(8,128)(2,1)S(1)}, bf16[32,2048]{1,0:T(8,128)(2,1)S(1)}, u32[]{:S(2)}, u32[]{:S(2)}) %collective-permute-start.9) | collective-permute-done | bytes 131104 | tf_op jit(solution)/shard_map/ppermute | solution.py:155
  44.1 1.5 %collective-permute-start.10 = (bf16[8,2048]{1,0:T(8,128)(2,1)S(1)}, bf16[8,2048]{1,0:T(8,128)(2,1)S(1)}, u32[]{:S(2)}, u32[]{:S(2)}) collective-permute-start(bf16[8,2048]{1,0:T(8,128)(2,1)S(1)} %get-tuple-element.43), channel_id=1, source_target_pairs={{0,8},{4,12},{8,0},{12,4},{1,9},{5,13},{9,1},{13,5},{2,10},{6,14},... | collective-permute-start | bytes 98312 | tf_op jit(solution)/shard_map/ppermute | solution.py:155
  45.5 1.4 %collective-permute-start.12 = (bf16[8,2048]{1,0:T(8,128)(2,1)S(1)}, bf16[8,2048]{1,0:T(8,128)(2,1)S(1)}, u32[]{:S(2)}, u32[]{:S(2)}) collective-permute-start(bf16[8,2048]{1,0:T(8,128)(2,1)S(1)} %get-tuple-element.44), channel_id=1, source_target_pairs={{0,12},{4,8},{8,4},{12,0},{1,13},{5,9},{9,5},{13,1},{2,14},{6,10},... | collective-permute-start | bytes 98312 | tf_op jit(solution)/shard_map/ppermute | solution.py:155
  47.0 0.7 %collective-permute-start.11 = (bf16[8,2048]{1,0:T(8,128)(2,1)S(1)}, bf16[8,2048]{1,0:T(8,128)(2,1)S(1)}, u32[]{:S(2)}, u32[]{:S(2)}) collective-permute-start(bf16[8,2048]{1,0:T(8,128)(2,1)S(1)} %get-tuple-element.45), channel_id=1, source_target_pairs={{0,4},{4,0},{8,12},{12,8},{1,5},{5,1},{9,13},{13,9},{2,6},{6,2},{1... | collective-permute-start | bytes 98312 | tf_op jit(solution)/shard_map/ppermute | solution.py:155
  47.6 1.7 %collective-permute-done.10 = bf16[8,2048]{1,0:T(8,128)(2,1)S(1)} collective-permute-done((bf16[8,2048]{1,0:T(8,128)(2,1)S(1)}, bf16[8,2048]{1,0:T(8,128)(2,1)S(1)}, u32[]{:S(2)}, u32[]{:S(2)}) %collective-permute-start.10) | collective-permute-done | bytes 32800 | tf_op jit(solution)/shard_map/ppermute | solution.py:155
  49.3 1.9 %collective-permute-done.12 = bf16[8,2048]{1,0:T(8,128)(2,1)S(1)} collective-permute-done((bf16[8,2048]{1,0:T(8,128)(2,1)S(1)}, bf16[8,2048]{1,0:T(8,128)(2,1)S(1)}, u32[]{:S(2)}, u32[]{:S(2)}) %collective-permute-start.12) | collective-permute-done | bytes 32800 | tf_op jit(solution)/shard_map/ppermute | solution.py:155
  51.2 0.0 collective-permute-done.11
  51.2 0.6 %fusion.2 = bf16[8,2048]{1,0:T(8,128)(2,1)} fusion(f32[32,2048]{1,0:T(8,128)S(1)} %get-tuple-element.42, bf16[8,2048]{1,0:T(8,128)(2,1)S(1)} %collective-permute-done.12, bf16[8,2048]{1,0:T(8,128)(2,1)S(1)} %collective-permute-done.11, bf16[8,2048]{1,0:T(8,128)(2,1)S(1)} %collective-permute-done.10), kind=kLoop, calls=%fused_computation.4 | loop fusion | flops 114688 | bytes 196608 | tf_op jit(solution)/shard_map/convert_element_type | solution.py:228
  (6 shorter events, 0.1 us)
Async XLA Ops:
  0.0 7.9 %copy-start = (bf16[8,2048]{1,0:T(8,128)(2,1)S(1)}, bf16[8,2048]{1,0:T(8,128)(2,1)}, u32[]{:S(2)}) copy-start(bf16[8,2048]{1,0:T(8,128)(2,1)} %refs_0_.6) | copy-start | bytes 98308
  0.0 7.9 %collective-permute-start = (bf16[8,2048]{1,0:T(8,128)(2,1)}, bf16[8,2048]{1,0:T(8,128)(2,1)S(1)}, u32[]{:S(2)}, u32[]{:S(2)}) collective-permute-start(bf16[8,2048]{1,0:T(8,128)(2,1)} %refs_0_.6), channel_id=1, source_target_pairs={{0,8},{4,12},{8,0},{12,4},{1,9},{5,13},{9,1},{13,5},{2,10},{6,14},... | collective-permute-start | bytes 98312 | tf_op jit(solution)/shard_map/ppermute | solution.py:155
  7.9 5.5 %collective-permute-start.1 = (bf16[16,2048]{1,0:T(8,128)(2,1)S(1)}, bf16[16,2048]{1,0:T(8,128)(2,1)S(1)}, u32[]{:S(2)}, u32[]{:S(2)}) collective-permute-start(bf16[16,2048]{1,0:T(8,128)(2,1)S(1)} %join.3.refs_2_.refs_0_), channel_id=1, source_target_pairs={{0,4},{4,0},{8,12},{12,8},{1,5},{5,1},{9,13},{13,9},{2,6},{6,2},{1... | collective-permute-start | bytes 196616 | tf_op jit(solution)/shard_map/ppermute | solution.py:155
  13.4 5.2 %collective-permute-start.2 = (bf16[32,2048]{1,0:T(8,128)(2,1)S(1)}, bf16[32,2048]{1,0:T(8,128)(2,1)S(1)}, u32[]{:S(2)}, u32[]{:S(2)}) collective-permute-start(bf16[32,2048]{1,0:T(8,128)(2,1)S(1)} %join.4.refs_4_.refs_0_), channel_id=1, source_target_pairs={{0,16},{16,0},{1,17},{17,1},{2,18},{18,2},{3,19},{19,3},{4,20},{20... | collective-permute-start | bytes 393224 | tf_op jit(solution)/shard_map/ppermute | solution.py:155
  20.3 1.8 %collective-permute-start.3 = (bf16[64,2304]{1,0:T(8,128)(2,1)S(1)}, bf16[64,2304]{1,0:T(8,128)(2,1)S(1)}, u32[]{:S(2)}, u32[]{:S(2)}) collective-permute-start(bf16[64,2304]{1,0:T(8,128)(2,1)S(1)} %send_0.1.refs_3_), channel_id=1, source_target_pairs={{0,1},{1,0},{2,3},{3,2},{4,5},{5,4},{6,7},{7,6},{8,9},{9,8},{10,11... | collective-permute-start | bytes 884744 | tf_op jit(solution)/shard_map/ppermute | solution.py:155
  22.3 9.9 %collective-permute-start.4 = (bf16[64,2304]{1,0:T(8,128)(2,1)S(1)}, bf16[64,2304]{1,0:T(8,128)(2,1)S(1)}, u32[]{:S(2)}, u32[]{:S(2)}) collective-permute-start(bf16[64,2304]{1,0:T(8,128)(2,1)S(1)} %get-tuple-element.29.refs_3_), channel_id=1, source_target_pairs={{0,2},{1,3},{2,0},{3,1},{4,6},{5,7},{6,4},{7,5},{8,10},{9,11},{10,... | collective-permute-start | bytes 884744 | tf_op jit(solution)/shard_map/ppermute | solution.py:155
  24.7 1.4 %collective-permute-start.5 = (bf16[64,1024]{1,0:T(8,128)(2,1)S(1)}, bf16[64,1024]{1,0:T(8,128)(2,1)S(1)}, u32[]{:S(2)}, u32[]{:S(2)}) collective-permute-start(bf16[64,1024]{1,0:T(8,128)(2,1)S(1)} %send_1.1.refs_3_), channel_id=1, source_target_pairs={{0,1},{1,0},{2,3},{3,2},{4,5},{5,4},{6,7},{7,6},{8,9},{9,8},{10,11... | collective-permute-start | bytes 393224 | tf_op jit(solution)/shard_map/ppermute | solution.py:155
  26.1 8.4 %collective-permute-start.7 = (bf16[64,1024]{1,0:T(8,128)(2,1)S(1)}, bf16[64,1024]{1,0:T(8,128)(2,1)S(1)}, u32[]{:S(2)}, u32[]{:S(2)}) collective-permute-start(bf16[64,1024]{1,0:T(8,128)(2,1)S(1)} %get-tuple-element.33.refs_4_), channel_id=1, source_target_pairs={{0,2},{1,3},{2,0},{3,1},{4,6},{5,7},{6,4},{7,5},{8,10},{9,11},{10,... | collective-permute-start | bytes 393224 | tf_op jit(solution)/shard_map/ppermute | solution.py:155
  32.3 2.4 %collective-permute-start.6 = (bf16[64,1152]{1,0:T(8,128)(2,1)S(1)}, bf16[64,1152]{1,0:T(8,128)(2,1)S(1)}, u32[]{:S(2)}, u32[]{:S(2)}) collective-permute-start(bf16[64,1152]{1,0:T(8,128)(2,1)S(1)} %hidden.2.refs_2_.refs_0_), channel_id=1, source_target_pairs={{0,1},{1,0},{2,3},{3,2},{4,5},{5,4},{6,7},{7,6},{8,9},{9,8},{10,11... | collective-permute-start | bytes 442376 | tf_op jit(solution)/shard_map/ppermute | solution.py:155
  34.6 2.2 %collective-permute-start.8 = (bf16[64,512]{1,0:T(8,128)(2,1)S(1)}, bf16[64,512]{1,0:T(8,128)(2,1)S(1)}, u32[]{:S(2)}, u32[]{:S(2)}) collective-permute-start(bf16[64,512]{1,0:T(8,128)(2,1)S(1)} %hidden.3.refs_4_.refs_1_), channel_id=1, source_target_pairs={{0,1},{1,0},{2,3},{3,2},{4,5},{5,4},{6,7},{7,6},{8,9},{9,8},{10,11... | collective-permute-start | bytes 196616 | tf_op jit(solution)/shard_map/ppermute | solution.py:155
  38.1 6.0 %collective-permute-start.9 = (bf16[32,2048]{1,0:T(8,128)(2,1)S(1)}, bf16[32,2048]{1,0:T(8,128)(2,1)S(1)}, u32[]{:S(2)}, u32[]{:S(2)}) collective-permute-start(bf16[32,2048]{1,0:T(8,128)(2,1)S(1)} %get-tuple-element.40), channel_id=1, source_target_pairs={{0,16},{16,0},{1,17},{17,1},{2,18},{18,2},{3,19},{19,3},{4,20},{20... | collective-permute-start | bytes 393224 | tf_op jit(solution)/shard_map/ppermute | solution.py:155
  44.1 5.2 %collective-permute-start.10 = (bf16[8,2048]{1,0:T(8,128)(2,1)S(1)}, bf16[8,2048]{1,0:T(8,128)(2,1)S(1)}, u32[]{:S(2)}, u32[]{:S(2)}) collective-permute-start(bf16[8,2048]{1,0:T(8,128)(2,1)S(1)} %get-tuple-element.43), channel_id=1, source_target_pairs={{0,8},{4,12},{8,0},{12,4},{1,9},{5,13},{9,1},{13,5},{2,10},{6,14},... | collective-permute-start | bytes 98312 | tf_op jit(solution)/shard_map/ppermute | solution.py:155
  45.5 5.7 %collective-permute-start.12 = (bf16[8,2048]{1,0:T(8,128)(2,1)S(1)}, bf16[8,2048]{1,0:T(8,128)(2,1)S(1)}, u32[]{:S(2)}, u32[]{:S(2)}) collective-permute-start(bf16[8,2048]{1,0:T(8,128)(2,1)S(1)} %get-tuple-element.44), channel_id=1, source_target_pairs={{0,12},{4,8},{8,4},{12,0},{1,13},{5,9},{9,5},{13,1},{2,14},{6,10},... | collective-permute-start | bytes 98312 | tf_op jit(solution)/shard_map/ppermute | solution.py:155
  47.0 4.3 %collective-permute-start.11 = (bf16[8,2048]{1,0:T(8,128)(2,1)S(1)}, bf16[8,2048]{1,0:T(8,128)(2,1)S(1)}, u32[]{:S(2)}, u32[]{:S(2)}) collective-permute-start(bf16[8,2048]{1,0:T(8,128)(2,1)S(1)} %get-tuple-element.45), channel_id=1, source_target_pairs={{0,4},{4,0},{8,12},{12,8},{1,5},{5,1},{9,13},{13,9},{2,6},{6,2},{1... | collective-permute-start | bytes 98312 | tf_op jit(solution)/shard_map/ppermute | solution.py:155

commit v6 on v5

--- a/solution.py
+++ b/solution.py
@@ -89,20 +89,20 @@
 
 
 def down_body(refs, out_refs):
-    *so_far, own_ref, other_ref, w_own, w_other = refs
+    n_pairs = len(refs) // 2
+    pairs = list(zip(refs[:n_pairs], refs[n_pairs : 2 * n_pairs]))
     size = 512
 
     def one(at):
         span = pl.ds(at, size)
-        got = jnp.dot(own_ref[...], w_own[:, span], preferred_element_type=F32)
-        got += jnp.dot(other_ref[...], w_other[:, span], preferred_element_type=F32)
-        for ref in so_far:
+        got = sum(jnp.dot(h_ref[...], w_ref[:, span], preferred_element_type=F32) for h_ref, w_ref in pairs)
+        for ref in refs[2 * n_pairs :]:
             got += ref[:, span]
         part = got.shape[0] // len(out_refs)
         for k, ref in enumerate(out_refs):
             ref[:, span] = got[k * part : (k + 1) * part].astype(ref.dtype)
 
-    each_tile(w_own.shape[1], size, one)
+    each_tile(pairs[0][1].shape[1], size, one)
 
 
 def sum_body(refs, out_refs):
@@ -199,7 +199,7 @@
     other = swap(x, "groups", n_groups, 1)
     g2s, u2s, g2k, u2k = step("fetch_2", None, [], [], both(1, False) + both(1, True), [x])
     x = join(x, other, g2s)
-    (send1,) = step("send_0", gate_up_body, [x, g1s, u1s], [sums(0, BF16)], [])
+    (send1,) = step("send_0", gate_up_body, [x, g1s, u1s], [sums(0, F32)], [])
     got1 = core_swap(send1)
     (keep1,) = step("keep_0", gate_up_body, [x, g1k, u1k], [sums(0, F32)], [], [send1])
     sum1, out1 = sum_of(keep1, got1)
@@ -212,12 +212,13 @@
     d1k, d1s, d2k, d2s = step("fetch_3", None, [], [], tall(0) + tall(1), [out2])
     h1 = hidden_of(sum1, crossed1, [d1k])
     h1_other = core_swap(h1)
-    h2 = hidden_of(sum2, crossed2, [h1])
+    whole, part = (rows, columns), (rows // 2, columns)
+    (so_far,) = step("down_0", down_body, [h1, d1k], [(whole, F32)], [])
+    h2 = hidden_of(sum2, crossed2, [so_far])
     h2_other = core_swap(h2)
-    (so_far,) = step("down_0", down_body, [h1, h1_other, d1k, d1s], [((rows, columns), F32)], [], [h2])
-    part = (rows // 2, columns)
+    (so_far,) = step("down_1", down_body, [h1_other, d1s, so_far], [(whole, F32)], [], [h2])
     own, send = step(
-        "down_1", down_body, [so_far, h2, h2_other, d2k, d2s], [(part, F32), (part, BF16)], []
+        "down_2", down_body, [h2, h2_other, d2k, d2s, so_far], [(part, F32), (part, BF16)], []
     )
     own = own + swap(send, "groups", n_groups, 1).astype(F32)
     few = tokens.shape[0]

time: 52 us -> 50.9 us (0.979)
  waiting for transfers between devices: 11 us -> 8.69 us
  starting transfers between devices: 15 us -> 15.6 us
    ppermute x13, waiting for transfers between devices: 11 us -> 8.69 us  [swap(): return lax.ppermute(array, axis, flip(size, bit))]
    ppermute x13, starting transfers between devices: 15 us -> 15.6 us  [swap(): return lax.ppermute(array, axis, flip(size, bit))]
    pallas_call x17 -> x18, Pallas kernels: 25 us -> 25.5 us  [step(): pl.pallas_call(kernel, out_shape=out_shape, in_specs=[VMEM] * n_in + [ANY...]
  transfers between devices with their start and end apart: 13 -> 13, of which waited for: 6 -> 7; matrix products, arithmetic and copies ran while one was open for 0% -> 0% of each run, Pallas kernels for 42% -> 44%
where the time goes in v6:
time: 50.9 us; the launch traced here: 50.7 us
  Pallas kernels  25.5 us (50%)
  starting transfers between devices  15.6 us (31%)
  waiting for transfers between devices  8.69 us (17%)
  other arithmetic  0.66 us (1%)
    pallas_call x18, Pallas kernels, step(): pl.pallas_call(kernel, out_shape=out_shape, in_specs=[VMEM] * n_in + [ANY...  25.5 us
    ppermute x13, starting transfers between devices, swap(): return lax.ppermute(array, axis, flip(size, bit))  15.6 us
    ppermute x13, waiting for transfers between devices, swap(): return lax.ppermute(array, axis, flip(size, bit))  8.69 us
  transfers between devices with their start and end apart: 13, of which 7 were waited for; matrix products, arithmetic and copies ran while one was open for 0% of the time, Pallas kernels for 44%

profile of v6, /device:TPU:0, one launch (start us, length us, event | category | flops | bytes accessed | tf_op | source)
XLA Modules:
  0.0 50.7 jit_solution(13617864582336955130)
XLA Ops:
  0.0 0.0 copy-start
  0.0 4.0 %collective-permute-start = (bf16[8,2048]{1,0:T(8,128)(2,1)}, bf16[8,2048]{1,0:T(8,128)(2,1)S(1)}, u32[]{:S(2)}, u32[]{:S(2)}) collective-permute-start(bf16[8,2048]{1,0:T(8,128)(2,1)} %refs_0_.6), channel_id=1, source_target_pairs={{0,8},{4,12},{8,0},{12,4},{1,9},{5,13},{9,1},{13,5},{2,10},{6,14},... | collective-permute-start | bytes 98312 | tf_op jit(solution)/shard_map/ppermute | solution.py:155
  4.0 3.8 %fetch_0.1 = (bf16[2048,1152]{1,0:T(8,128)(2,1)S(1)}, bf16[2048,1152]{1,0:T(8,128)(2,1)S(1)}) custom-call(bf16[2048,6656]{1,0:T(8,128)(2,1)} %refs_2_.2, bf16[2048,6656]{1,0:T(8,128)(2,1)} %refs_3_.2), custom_call_target="tpu_custom_call" | custom-call | flops 1000 | bytes 1000 | tf_op jit(solution)/shard_map/fetch_0/pallas_call | solution.py:57
  7.9 0.0 collective-permute-done.refs_1_
  7.9 0.0 copy-done
  7.9 1.6 %collective-permute-start.1 = (bf16[16,2048]{1,0:T(8,128)(2,1)S(1)}, bf16[16,2048]{1,0:T(8,128)(2,1)S(1)}, u32[]{:S(2)}, u32[]{:S(2)}) collective-permute-start(bf16[16,2048]{1,0:T(8,128)(2,1)S(1)} %join.3.refs_2_.refs_0_), channel_id=1, source_target_pairs={{0,4},{4,0},{8,12},{12,8},{1,5},{5,1},{9,13},{13,9},{2,6},{6,2},{1... | collective-permute-start | bytes 196616 | tf_op jit(solution)/shard_map/ppermute | solution.py:155
  9.5 3.8 %fetch_1.1 = (bf16[2048,1152]{1,0:T(8,128)(2,1)S(1)}, bf16[2048,1152]{1,0:T(8,128)(2,1)S(1)}) custom-call(bf16[2048,6656]{1,0:T(8,128)(2,1)} %refs_2_.2, bf16[2048,6656]{1,0:T(8,128)(2,1)} %refs_3_.2, bf16[16,2048]{1,0:T(8,128)(2,1)S(1)} %join.3.refs_2_.refs_0_), custom_call_target="tpu_custom_call" | custom-call | flops 1000 | bytes 1000 | tf_op jit(solution)/shard_map/fetch_1/pallas_call | solution.py:57
  13.4 0.0 collective-permute-done.1.refs_1_
  13.4 1.6 %collective-permute-start.2 = (bf16[32,2048]{1,0:T(8,128)(2,1)S(1)}, bf16[32,2048]{1,0:T(8,128)(2,1)S(1)}, u32[]{:S(2)}, u32[]{:S(2)}) collective-permute-start(bf16[32,2048]{1,0:T(8,128)(2,1)S(1)} %join.4.refs_4_.refs_0_), channel_id=1, source_target_pairs={{0,16},{16,0},{1,17},{17,1},{2,18},{18,2},{3,19},{19,3},{4,20},{20... | collective-permute-start | bytes 393224 | tf_op jit(solution)/shard_map/ppermute | solution.py:155
  15.0 3.5 %fetch_2.1 = (bf16[2048,512]{1,0:T(8,128)(2,1)S(1)}, bf16[2048,512]{1,0:T(8,128)(2,1)S(1)}, bf16[2048,512]{1,0:T(8,128)(2,1)S(1)}, bf16[2048,512]{1,0:T(8,128)(2,1)S(1)}) custom-call(bf16[2048,6656]{1,0:T(8,128)(2,1)} %refs_2_.2, bf16[2048,6656]{1,0:T(8,128)(2,1)} %refs_3_.2, bf16[2048,6656]{1,0:T(8,128)(2,1)} %refs_2_.2, bf16[2048,6656]{1,0:T(8,128)(2,1)} %refs_3_.2, ...), custom_call_target="tpu_custom_call" | custom-call | flops 1000 | bytes 1000 | tf_op jit(solution)/shard_map/fetch_2/pallas_call | solution.py:57
  18.6 0.0 collective-permute-done.2.refs_1_
  18.6 1.7 %send_0.1.refs_3_ = f32[64,2304]{1,0:T(8,128)S(1)} custom-call(bf16[64,2048]{1,0:T(8,128)(2,1)S(1)} %join.5.refs_0_, bf16[2048,1152]{1,0:T(8,128)(2,1)S(1)} %get-tuple-element.23.refs_2_.refs_1_, bf16[2048,1152]{1,0:T(8,128)(2,1)S(1)} %get-tuple-element.30.refs_2_), custom_call_target="tpu_custom_call" | custom-call | flops 1000 | bytes 1000 | tf_op jit(solution)/shard_map/send_0/pallas_call | solution.py:57
  20.3 0.1 collective-permute-start.3
  20.4 1.7 %keep_0.1.refs_0_ = f32[64,2304]{1,0:T(8,128)S(1)} custom-call(bf16[64,2048]{1,0:T(8,128)(2,1)S(1)} %join.5.refs_0_, bf16[2048,1152]{1,0:T(8,128)(2,1)S(1)} %get-tuple-element.24.refs_2_.refs_1_, bf16[2048,1152]{1,0:T(8,128)(2,1)S(1)} %get-tuple-element.29.refs_2_, f32[64,2304]{1,0:T(8,128)S(1)} %send_0.1.refs_3_), custom_call_target="tpu_custom_call" | custom-call | flops 1000 | bytes 1000 | tf_op jit(solution)/shard_map/keep_0/pallas_call | solution.py:57
  22.2 0.2 collective-permute-done.3.refs_1_
  22.4 0.1 sum.2
  22.5 1.6 %collective-permute-start.6 = (bf16[64,2304]{1,0:T(8,128)(2,1)S(1)}, bf16[64,2304]{1,0:T(8,128)(2,1)S(1)}, u32[]{:S(2)}, u32[]{:S(2)}) collective-permute-start(bf16[64,2304]{1,0:T(8,128)(2,1)S(1)} %get-tuple-element.31.refs_3_), channel_id=1, source_target_pairs={{0,2},{1,3},{2,0},{3,1},{4,6},{5,7},{6,4},{7,5},{8,10},{9,11},{10,... | collective-permute-start | bytes 884744 | tf_op jit(solution)/shard_map/ppermute | solution.py:155
  24.0 0.8 %send_1.1.refs_3_ = bf16[64,1024]{1,0:T(8,128)(2,1)S(1)} custom-call(bf16[64,2048]{1,0:T(8,128)(2,1)S(1)} %join.5.refs_0_, bf16[2048,512]{1,0:T(8,128)(2,1)S(1)} %get-tuple-element.25.refs_2_.refs_1_, bf16[2048,512]{1,0:T(8,128)(2,1)S(1)} %get-tuple-element.28.refs_2_, bf16[64,2304]{1,0:T(8,128)(2,1)S(1)} %get-tuple-element.31.refs_3_), custom_call_target="tpu_custom_call" | custom-call | flops 1000 | bytes 1000 | tf_op jit(solution)/shard_map/send_1/pallas_call | solution.py:57
  24.9 0.1 collective-permute-start.4
  25.0 0.8 %keep_1.1.refs_0_ = f32[64,1024]{1,0:T(8,128)S(1)} custom-call(bf16[64,2048]{1,0:T(8,128)(2,1)S(1)} %join.5.refs_0_, bf16[2048,512]{1,0:T(8,128)(2,1)S(1)} %get-tuple-element.26.refs_1_, bf16[2048,512]{1,0:T(8,128)(2,1)S(1)} %get-tuple-element.27.refs_2_, bf16[64,1024]{1,0:T(8,128)(2,1)S(1)} %send_1.1.refs_3_), custom_call_target="tpu_custom_call" | custom-call | flops 1000 | bytes 1000 | tf_op jit(solution)/shard_map/keep_1/pallas_call | solution.py:57
  25.8 0.5 collective-permute-done.4.refs_1_
  26.3 0.6 %collective-permute-start.5 = (bf16[64,1024]{1,0:T(8,128)(2,1)S(1)}, bf16[64,1024]{1,0:T(8,128)(2,1)S(1)}, u32[]{:S(2)}, u32[]{:S(2)}) collective-permute-start(bf16[64,1024]{1,0:T(8,128)(2,1)S(1)} %get-tuple-element.33.refs_4_), channel_id=1, source_target_pairs={{0,2},{1,3},{2,0},{3,1},{4,6},{5,7},{6,4},{7,5},{8,10},{9,11},{10,... | collective-permute-start | bytes 393224 | tf_op jit(solution)/shard_map/ppermute | solution.py:155
  26.9 5.0 %fetch_3.1 = (bf16[1152,2048]{1,0:T(8,128)(2,1)S(1)}, bf16[1152,2048]{1,0:T(8,128)(2,1)S(1)}, bf16[512,2048]{1,0:T(8,128)(2,1)S(1)}, bf16[512,2048]{1,0:T(8,128)(2,1)S(1)}) custom-call(bf16[6656,2048]{1,0:T(8,128)(2,1)} %refs_3_.3, bf16[6656,2048]{1,0:T(8,128)(2,1)} %refs_3_.3, bf16[6656,2048]{1,0:T(8,128)(2,1)} %refs_3_.3, bf16[6656,2048]{1,0:T(8,128)(2,1)} %refs_3_.3, ...), custom_call_target="tpu_custom_call" | custom-call | flops 1000 | bytes 1000 | tf_op jit(solution)/shard_map/fetch_3/pallas_call | solution.py:57
  31.9 0.4 collective-permute-done.6.refs_1_
  32.4 0.1 hidden.2.refs_0_
  32.5 0.1 collective-permute-start.8
  32.6 1.3 %down_0.1.refs_2_ = f32[64,2048]{1,0:T(8,128)S(1)} custom-call(bf16[64,1152]{1,0:T(8,128)(2,1)S(1)} %hidden.2.refs_0_, bf16[1152,2048]{1,0:T(8,128)(2,1)S(1)} %get-tuple-element.35.refs_2_.refs_1_), custom_call_target="tpu_custom_call" | custom-call | flops 1000 | bytes 1000 | tf_op jit(solution)/shard_map/down_0/pallas_call | solution.py:57
  33.9 0.6 %collective-permute-done.5.refs_1_ = bf16[64,1024]{1,0:T(8,128)(2,1)S(1)} collective-permute-done((bf16[64,1024]{1,0:T(8,128)(2,1)S(1)}, bf16[64,1024]{1,0:T(8,128)(2,1)S(1)}, u32[]{:S(2)}, u32[]{:S(2)}) %collective-permute-start.5) | collective-permute-done | bytes 131104 | tf_op jit(solution)/shard_map/ppermute | solution.py:155
  34.5 0.1 hidden.3.refs_3_.refs_0_
  34.6 0.1 collective-permute-start.7
  34.7 0.0 collective-permute-done.8.refs_0_
  34.7 1.3 %down_1.1.refs_4_ = f32[64,2048]{1,0:T(8,128)S(1)} custom-call(bf16[64,1152]{1,0:T(8,128)(2,1)S(1)} %collective-permute-done.8.refs_0_, bf16[1152,2048]{1,0:T(8,128)(2,1)S(1)} %get-tuple-element.38.refs_1_, f32[64,2048]{1,0:T(8,128)S(1)} %down_0.1.refs_2_, bf16[64,512]{1,0:T(8,128)(2,1)S(1)} %hidden.3.refs_3_.refs_0_), custom_call_target="tpu_custom_call" | custom-call | flops 1000 | bytes 1000 | tf_op jit(solution)/shard_map/down_1/pallas_call | solution.py:57
  36.0 0.0 collective-permute-done.7.refs_1_
  36.0 1.2 %down_2.1 = (f32[32,2048]{1,0:T(8,128)S(1)}, bf16[32,2048]{1,0:T(8,128)(2,1)S(1)}) custom-call(bf16[64,512]{1,0:T(8,128)(2,1)S(1)} %hidden.3.refs_3_.refs_0_, bf16[64,512]{1,0:T(8,128)(2,1)S(1)} %collective-permute-done.7.refs_1_, bf16[512,2048]{1,0:T(8,128)(2,1)S(1)} %get-tuple-element.36.refs_2_, bf16[512,2048]{1,0:T(8,128)(2,1)S(1)} %get-tuple-element.37.refs_3_, ...), custom_call_target="tpu_custom_call" | custom-call | flops 1000 | bytes 1000 | tf_op jit(solution)/shard_map/down_2/pallas_call | solution.py:57
  37.3 1.5 %collective-permute-start.9 = (bf16[32,2048]{1,0:T(8,128)(2,1)S(1)}, bf16[32,2048]{1,0:T(8,128)(2,1)S(1)}, u32[]{:S(2)}, u32[]{:S(2)}) collective-permute-start(bf16[32,2048]{1,0:T(8,128)(2,1)S(1)} %get-tuple-element.40), channel_id=1, source_target_pairs={{0,16},{16,0},{1,17},{17,1},{2,18},{18,2},{3,19},{19,3},{4,20},{20... | collective-permute-start | bytes 393224 | tf_op jit(solution)/shard_map/ppermute | solution.py:155
  38.7 4.5 %collective-permute-done.9 = bf16[32,2048]{1,0:T(8,128)(2,1)S(1)} collective-permute-done((bf16[32,2048]{1,0:T(8,128)(2,1)S(1)}, bf16[32,2048]{1,0:T(8,128)(2,1)S(1)}, u32[]{:S(2)}, u32[]{:S(2)}) %collective-permute-start.9) | collective-permute-done | bytes 131104 | tf_op jit(solution)/shard_map/ppermute | solution.py:155
  43.3 1.3 %collective-permute-start.12 = (bf16[8,2048]{1,0:T(8,128)(2,1)S(1)}, bf16[8,2048]{1,0:T(8,128)(2,1)S(1)}, u32[]{:S(2)}, u32[]{:S(2)}) collective-permute-start(bf16[8,2048]{1,0:T(8,128)(2,1)S(1)} %get-tuple-element.44), channel_id=1, source_target_pairs={{0,12},{4,8},{8,4},{12,0},{1,13},{5,9},{9,5},{13,1},{2,14},{6,10},... | collective-permute-start | bytes 98312 | tf_op jit(solution)/shard_map/ppermute | solution.py:155
  44.6 0.7 %collective-permute-start.11 = (bf16[8,2048]{1,0:T(8,128)(2,1)S(1)}, bf16[8,2048]{1,0:T(8,128)(2,1)S(1)}, u32[]{:S(2)}, u32[]{:S(2)}) collective-permute-start(bf16[8,2048]{1,0:T(8,128)(2,1)S(1)} %get-tuple-element.45), channel_id=1, source_target_pairs={{0,4},{4,0},{8,12},{12,8},{1,5},{5,1},{9,13},{13,9},{2,6},{6,2},{1... | collective-permute-start | bytes 98312 | tf_op jit(solution)/shard_map/ppermute | solution.py:155
  45.3 2.4 %collective-permute-start.10 = (bf16[8,2048]{1,0:T(8,128)(2,1)S(1)}, bf16[8,2048]{1,0:T(8,128)(2,1)S(1)}, u32[]{:S(2)}, u32[]{:S(2)}) collective-permute-start(bf16[8,2048]{1,0:T(8,128)(2,1)S(1)} %get-tuple-element.43), channel_id=1, source_target_pairs={{0,8},{4,12},{8,0},{12,4},{1,9},{5,13},{9,1},{13,5},{2,10},{6,14},... | collective-permute-start | bytes 98312 | tf_op jit(solution)/shard_map/ppermute | solution.py:155
  47.7 1.7 %collective-permute-done.12 = bf16[8,2048]{1,0:T(8,128)(2,1)S(1)} collective-permute-done((bf16[8,2048]{1,0:T(8,128)(2,1)S(1)}, bf16[8,2048]{1,0:T(8,128)(2,1)S(1)}, u32[]{:S(2)}, u32[]{:S(2)}) %collective-permute-start.12) | collective-permute-done | bytes 32800 | tf_op jit(solution)/shard_map/ppermute | solution.py:155
  49.4 0.0 collective-permute-done.11
  49.4 0.7 %collective-permute-done.10 = bf16[8,2048]{1,0:T(8,128)(2,1)S(1)} collective-permute-done((bf16[8,2048]{1,0:T(8,128)(2,1)S(1)}, bf16[8,2048]{1,0:T(8,128)(2,1)S(1)}, u32[]{:S(2)}, u32[]{:S(2)}) %collective-permute-start.10) | collective-permute-done | bytes 32800 | tf_op jit(solution)/shard_map/ppermute | solution.py:155
  50.1 0.6 %fusion.2 = bf16[8,2048]{1,0:T(8,128)(2,1)} fusion(f32[32,2048]{1,0:T(8,128)S(1)} %get-tuple-element.42, bf16[8,2048]{1,0:T(8,128)(2,1)S(1)} %collective-permute-done.12, bf16[8,2048]{1,0:T(8,128)(2,1)S(1)} %collective-permute-done.11, bf16[8,2048]{1,0:T(8,128)(2,1)S(1)} %collective-permute-done.10), kind=kLoop, calls=%fused_computation.4 | loop fusion | flops 114688 | bytes 196608 | tf_op jit(solution)/shard_map/convert_element_type | solution.py:229
  (6 shorter events, 0.1 us)
Async XLA Ops:
  0.0 7.9 %copy-start = (bf16[8,2048]{1,0:T(8,128)(2,1)S(1)}, bf16[8,2048]{1,0:T(8,128)(2,1)}, u32[]{:S(2)}) copy-start(bf16[8,2048]{1,0:T(8,128)(2,1)} %refs_0_.6) | copy-start | bytes 98308
  0.0 7.9 %collective-permute-start = (bf16[8,2048]{1,0:T(8,128)(2,1)}, bf16[8,2048]{1,0:T(8,128)(2,1)S(1)}, u32[]{:S(2)}, u32[]{:S(2)}) collective-permute-start(bf16[8,2048]{1,0:T(8,128)(2,1)} %refs_0_.6), channel_id=1, source_target_pairs={{0,8},{4,12},{8,0},{12,4},{1,9},{5,13},{9,1},{13,5},{2,10},{6,14},... | collective-permute-start | bytes 98312 | tf_op jit(solution)/shard_map/ppermute | solution.py:155
  7.9 5.5 %collective-permute-start.1 = (bf16[16,2048]{1,0:T(8,128)(2,1)S(1)}, bf16[16,2048]{1,0:T(8,128)(2,1)S(1)}, u32[]{:S(2)}, u32[]{:S(2)}) collective-permute-start(bf16[16,2048]{1,0:T(8,128)(2,1)S(1)} %join.3.refs_2_.refs_0_), channel_id=1, source_target_pairs={{0,4},{4,0},{8,12},{12,8},{1,5},{5,1},{9,13},{13,9},{2,6},{6,2},{1... | collective-permute-start | bytes 196616 | tf_op jit(solution)/shard_map/ppermute | solution.py:155
  13.4 5.2 %collective-permute-start.2 = (bf16[32,2048]{1,0:T(8,128)(2,1)S(1)}, bf16[32,2048]{1,0:T(8,128)(2,1)S(1)}, u32[]{:S(2)}, u32[]{:S(2)}) collective-permute-start(bf16[32,2048]{1,0:T(8,128)(2,1)S(1)} %join.4.refs_4_.refs_0_), channel_id=1, source_target_pairs={{0,16},{16,0},{1,17},{17,1},{2,18},{18,2},{3,19},{19,3},{4,20},{20... | collective-permute-start | bytes 393224 | tf_op jit(solution)/shard_map/ppermute | solution.py:155
  20.3 2.1 %collective-permute-start.3 = (f32[64,2304]{1,0:T(8,128)S(1)}, f32[64,2304]{1,0:T(8,128)S(1)}, u32[]{:S(2)}, u32[]{:S(2)}) collective-permute-start(f32[64,2304]{1,0:T(8,128)S(1)} %send_0.1.refs_3_), channel_id=1, source_target_pairs={{0,1},{1,0},{2,3},{3,2},{4,5},{5,4},{6,7},{7,6},{8,9},{9,8},{10,11... | collective-permute-start | bytes 1769480 | tf_op jit(solution)/shard_map/ppermute | solution.py:155
  22.5 9.9 %collective-permute-start.6 = (bf16[64,2304]{1,0:T(8,128)(2,1)S(1)}, bf16[64,2304]{1,0:T(8,128)(2,1)S(1)}, u32[]{:S(2)}, u32[]{:S(2)}) collective-permute-start(bf16[64,2304]{1,0:T(8,128)(2,1)S(1)} %get-tuple-element.31.refs_3_), channel_id=1, source_target_pairs={{0,2},{1,3},{2,0},{3,1},{4,6},{5,7},{6,4},{7,5},{8,10},{9,11},{10,... | collective-permute-start | bytes 884744 | tf_op jit(solution)/shard_map/ppermute | solution.py:155
  24.9 1.4 %collective-permute-start.4 = (bf16[64,1024]{1,0:T(8,128)(2,1)S(1)}, bf16[64,1024]{1,0:T(8,128)(2,1)S(1)}, u32[]{:S(2)}, u32[]{:S(2)}) collective-permute-start(bf16[64,1024]{1,0:T(8,128)(2,1)S(1)} %send_1.1.refs_3_), channel_id=1, source_target_pairs={{0,1},{1,0},{2,3},{3,2},{4,5},{5,4},{6,7},{7,6},{8,9},{9,8},{10,11... | collective-permute-start | bytes 393224 | tf_op jit(solution)/shard_map/ppermute | solution.py:155
  26.3 8.2 %collective-permute-start.5 = (bf16[64,1024]{1,0:T(8,128)(2,1)S(1)}, bf16[64,1024]{1,0:T(8,128)(2,1)S(1)}, u32[]{:S(2)}, u32[]{:S(2)}) collective-permute-start(bf16[64,1024]{1,0:T(8,128)(2,1)S(1)} %get-tuple-element.33.refs_4_), channel_id=1, source_target_pairs={{0,2},{1,3},{2,0},{3,1},{4,6},{5,7},{6,4},{7,5},{8,10},{9,11},{10,... | collective-permute-start | bytes 393224 | tf_op jit(solution)/shard_map/ppermute | solution.py:155
  32.5 2.2 %collective-permute-start.8 = (bf16[64,1152]{1,0:T(8,128)(2,1)S(1)}, bf16[64,1152]{1,0:T(8,128)(2,1)S(1)}, u32[]{:S(2)}, u32[]{:S(2)}) collective-permute-start(bf16[64,1152]{1,0:T(8,128)(2,1)S(1)} %hidden.2.refs_0_), channel_id=1, source_target_pairs={{0,1},{1,0},{2,3},{3,2},{4,5},{5,4},{6,7},{7,6},{8,9},{9,8},{10,11... | collective-permute-start | bytes 442376 | tf_op jit(solution)/shard_map/ppermute | solution.py:155
  34.6 1.4 %collective-permute-start.7 = (bf16[64,512]{1,0:T(8,128)(2,1)S(1)}, bf16[64,512]{1,0:T(8,128)(2,1)S(1)}, u32[]{:S(2)}, u32[]{:S(2)}) collective-permute-start(bf16[64,512]{1,0:T(8,128)(2,1)S(1)} %hidden.3.refs_3_.refs_0_), channel_id=1, source_target_pairs={{0,1},{1,0},{2,3},{3,2},{4,5},{5,4},{6,7},{7,6},{8,9},{9,8},{10,11... | collective-permute-start | bytes 196616 | tf_op jit(solution)/shard_map/ppermute | solution.py:155
  37.3 6.0 %collective-permute-start.9 = (bf16[32,2048]{1,0:T(8,128)(2,1)S(1)}, bf16[32,2048]{1,0:T(8,128)(2,1)S(1)}, u32[]{:S(2)}, u32[]{:S(2)}) collective-permute-start(bf16[32,2048]{1,0:T(8,128)(2,1)S(1)} %get-tuple-element.40), channel_id=1, source_target_pairs={{0,16},{16,0},{1,17},{17,1},{2,18},{18,2},{3,19},{19,3},{4,20},{20... | collective-permute-start | bytes 393224 | tf_op jit(solution)/shard_map/ppermute | solution.py:155
  43.3 6.1 %collective-permute-start.12 = (bf16[8,2048]{1,0:T(8,128)(2,1)S(1)}, bf16[8,2048]{1,0:T(8,128)(2,1)S(1)}, u32[]{:S(2)}, u32[]{:S(2)}) collective-permute-start(bf16[8,2048]{1,0:T(8,128)(2,1)S(1)} %get-tuple-element.44), channel_id=1, source_target_pairs={{0,12},{4,8},{8,4},{12,0},{1,13},{5,9},{9,5},{13,1},{2,14},{6,10},... | collective-permute-start | bytes 98312 | tf_op jit(solution)/shard_map/ppermute | solution.py:155
  44.6 4.8 %collective-permute-start.11 = (bf16[8,2048]{1,0:T(8,128)(2,1)S(1)}, bf16[8,2048]{1,0:T(8,128)(2,1)S(1)}, u32[]{:S(2)}, u32[]{:S(2)}) collective-permute-start(bf16[8,2048]{1,0:T(8,128)(2,1)S(1)} %get-tuple-element.45), channel_id=1, source_target_pairs={{0,4},{4,0},{8,12},{12,8},{1,5},{5,1},{9,13},{13,9},{2,6},{6,2},{1... | collective-permute-start | bytes 98312 | tf_op jit(solution)/shard_map/ppermute | solution.py:155
  45.3 4.8 %collective-permute-start.10 = (bf16[8,2048]{1,0:T(8,128)(2,1)S(1)}, bf16[8,2048]{1,0:T(8,128)(2,1)S(1)}, u32[]{:S(2)}, u32[]{:S(2)}) collective-permute-start(bf16[8,2048]{1,0:T(8,128)(2,1)S(1)} %get-tuple-element.43), channel_id=1, source_target_pairs={{0,8},{4,12},{8,0},{12,4},{1,9},{5,13},{9,1},{13,5},{2,10},{6,14},... | collective-permute-start | bytes 98312 | tf_op jit(solution)/shard_map/ppermute | solution.py:155
